TPU v7x, 128 devices: a whole 4x4x4 slice. The times are simulated.
128 devices in a mesh: tm: 16 (over x, y_lo, core), sta: 8 (over y_hi, z).
Axes of the slice: x: 4, y: 4 (y_hi: 2, y_lo: 2; y = y_hi * 2 + y_lo), z: 4, core: 2. Of those that a mesh axis runs over, the one named last changes fastest.
Arguments:
- records: bfloat16 [16, 3, 8192], P('sta', None, 'tm'), may hold values from -6 to 6
- templates: bfloat16 [128, 16, 3, 200], P('tm', 'sta'), may hold values from -0.25 to 0.25
- moveouts: int32 [128, 16], P(None, 'sta'), may hold values from 0 to 184, as said below
Outputs:
- detection: float32 [128, 8192], P('sta', 'tm')
Inputs may be any that keep to these rules, and one draw needn't show every extreme that they name: `moveouts`: for every template, some station has moveout 0 and some station has moveout 184.
All inputs are finite; a program needn't handle non-finite values.
Results may differ from a plain program's by a relative error of at most 0.0003.
Values may be sent and summed in bfloat16 or wider, within the bound.
No kernel may reach another device: no remote copies, remote signals or barrier semaphores. Data moves between devices by JAX's collectives and lax.ppermute only.
A program may use at most 64 MiB of HBM per device.

v0:
```python
import jax
import jax.numpy as jnp
from jax import lax
from jax.sharding import PartitionSpec as P

HALO = 384


EPS = 1e-06


def shifted(value, axis, steps):
    count = lax.axis_size(axis)
    first, last = (max(0, -steps), min(count, count - steps))
    return lax.ppermute(value, axis, [(source, source + steps) for source in range(first, last)])


def energy_inverse(extended, length):
    wide = extended.astype(jnp.float32)
    squares = jnp.sum(wide * wide, axis=1)
    energy = lax.reduce_window(squares, jnp.float32(0.0), lax.add, (1, length), (1, 1), "VALID")
    return lax.rsqrt(energy + EPS)


def lagged_windows(extended, length):
    stations = extended.shape[0]
    reach = extended.shape[2] - length + 1
    lagged = jnp.stack([extended[:, :, lag : lag + reach] for lag in range(length)], axis=2)
    return lagged.reshape(stations, 3 * length, reach)


def window_at(series, offset, extent):
    return lax.dynamic_slice_in_dim(series, offset, extent, 0)


def correlate(windows, inverse, waveforms, shifts, extent):
    stations = windows.shape[0]
    members = waveforms.shape[0]
    kernel = jnp.transpose(waveforms, (1, 0, 2, 3)).reshape(stations, members, windows.shape[1])
    correlations = jnp.einsum("sml,sle->sme", kernel, windows, preferred_element_type=jnp.float32)
    scaled = correlations * inverse[:, None, :]
    offsets = jnp.transpose(shifts)
    picked = jax.vmap(jax.vmap(lambda series, offset: window_at(series, offset, extent)))(
        scaled, offsets
    )
    return jnp.sum(picked, axis=0)


def local(records, templates, moveouts):
    extent = records.shape[2]
    length = templates.shape[3]
    following = shifted(records[:, :, :HALO], "tm", -1)
    extended = jnp.concatenate([records, following], axis=2)
    inverse = energy_inverse(extended, length)
    windows = lagged_windows(extended, length)
    everyone = templates.shape[0] * lax.axis_size("tm")
    empty = jnp.zeros((everyone, extent), jnp.float32)
    block_sums = correlate(
        windows, inverse, lax.all_gather(templates, "tm", axis=0, tiled=True), moveouts, extent
    )
    partial_sums = lax.dynamic_update_slice_in_dim(empty, block_sums, jnp.int32(0), 0)
    return lax.psum_scatter(partial_sums, "sta", scatter_dimension=0, tiled=True)


def solution(mesh):
    return jax.shard_map(
        local,
        mesh=mesh,
        in_specs=(P("sta", None, "tm"), P("tm", "sta", None, None), P(None, "sta")),
        out_specs=P("sta", "tm"),
        check_vma=False,
    )
```

profile of v0, /device:TPU:1, one launch (start us, length us, event | category | flops | bytes accessed | tf_op | source)
XLA Modules:
  0.0 837.9 jit_solution(3962149763636741288)
XLA Ops:
  7.2 3.3 collective-permute-start
  11.3 20.9 %all_gather.3 = bf16[128,2,3,200]{3,1,2,0:T(2,128)(2,1)S(1)} all-gather(bf16[8,2,3,200]{3,1,2,0:T(2,128)(2,1)} %param.4), channel_id=1, replica_groups=mesh['tm'=16,'sta'=8] {'tm'}, dimensions={0}, use_global_device_ids=true | all-gather | bytes 326400 | tf_op jit(solution)/shard_map/all_gather | solution.py:59
  51.9 19.3 %reduce_window.7 = f32[2,697]{1,0:T(2,128)S(1)} reduce-window(f32[2,896]{1,0:T(2,128)S(1)} %multiply_reduce_fusion, f32[]{:T(128)} %constant.0.clone.1), window={size=1x200}, to_apply=%region_1.0 | reduce-window | flops 277406 | bytes 12748 | tf_op jit(solution)/shard_map/reduce_window | solution.py:21
  72.4 690.4 %while.1 = (s32[]{:T(128)}, f32[2,128,697]{2,1,0:T(8,128)S(1)}, s32[256,3]{0,1:T(4,128)S(1)}, f32[256,512]{1,0:T(8,128)S(1)}, s32[]{:T(128)}, /*index=5*/s32[]{:T(128)}) while((s32[]{:T(128)}, f32[2,128,697]{2,1,0:T(8,128)S(1)}, s32[256,3]{0,1:T(4,128)S(1)}, f32[256,512]{1,0:T(8,128)S(1)}, s32[]{:T(128)}, /*index=5*/s32[]{:T(128)}) %tuple.28), condition=%wide.while_cond, body=%wide.while_body.sunk | while | flops 2 | bytes 8329 | solution.py:33
  73.1 2.0 dynamic-slice_bitcast_fusion.2
  75.8 2.0 dynamic-slice_bitcast_fusion.2
  78.5 2.0 dynamic-slice_bitcast_fusion.2
  81.2 2.0 dynamic-slice_bitcast_fusion.2
  83.9 2.0 dynamic-slice_bitcast_fusion.2
  86.6 2.0 dynamic-slice_bitcast_fusion.2
  89.3 2.0 dynamic-slice_bitcast_fusion.2
  92.0 2.0 dynamic-slice_bitcast_fusion.2
  94.7 2.0 dynamic-slice_bitcast_fusion.2
  97.4 2.0 dynamic-slice_bitcast_fusion.2
  100.1 2.0 dynamic-slice_bitcast_fusion.2
  102.8 2.0 dynamic-slice_bitcast_fusion.2
  105.5 2.0 dynamic-slice_bitcast_fusion.2
  108.2 2.0 dynamic-slice_bitcast_fusion.2
  110.9 2.0 dynamic-slice_bitcast_fusion.2
  113.6 2.0 dynamic-slice_bitcast_fusion.2
  119.0 2.0 dynamic-slice_bitcast_fusion.2
  121.6 2.0 dynamic-slice_bitcast_fusion.2
  124.3 2.0 dynamic-slice_bitcast_fusion.2
  127.0 2.0 dynamic-slice_bitcast_fusion.2
  129.7 2.0 dynamic-slice_bitcast_fusion.2
  132.4 2.0 dynamic-slice_bitcast_fusion.2
  135.1 2.0 dynamic-slice_bitcast_fusion.2
  137.8 2.0 dynamic-slice_bitcast_fusion.2
  140.5 2.0 dynamic-slice_bitcast_fusion.2
  143.2 2.0 dynamic-slice_bitcast_fusion.2
  145.9 2.0 dynamic-slice_bitcast_fusion.2
  148.6 2.0 dynamic-slice_bitcast_fusion.2
  151.3 2.0 dynamic-slice_bitcast_fusion.2
  154.0 2.0 dynamic-slice_bitcast_fusion.2
  156.7 2.0 dynamic-slice_bitcast_fusion.2
  159.4 2.0 dynamic-slice_bitcast_fusion.2
  162.1 2.0 dynamic-slice_bitcast_fusion.2
  164.8 2.0 dynamic-slice_bitcast_fusion.2
  170.2 2.0 dynamic-slice_bitcast_fusion.2
  172.9 2.0 dynamic-slice_bitcast_fusion.2
  175.6 2.0 dynamic-slice_bitcast_fusion.2
  178.3 2.0 dynamic-slice_bitcast_fusion.2
  181.0 2.0 dynamic-slice_bitcast_fusion.2
  183.7 2.0 dynamic-slice_bitcast_fusion.2
  186.4 2.0 dynamic-slice_bitcast_fusion.2
  189.1 2.0 dynamic-slice_bitcast_fusion.2
  191.8 2.0 dynamic-slice_bitcast_fusion.2
  194.5 2.0 dynamic-slice_bitcast_fusion.2
  197.2 2.0 dynamic-slice_bitcast_fusion.2
  199.9 2.0 dynamic-slice_bitcast_fusion.2
  202.6 2.0 dynamic-slice_bitcast_fusion.2
  205.2 2.0 dynamic-slice_bitcast_fusion.2
  207.9 2.0 dynamic-slice_bitcast_fusion.2
  210.6 2.0 dynamic-slice_bitcast_fusion.2
  213.3 2.0 dynamic-slice_bitcast_fusion.2
  216.0 2.0 dynamic-slice_bitcast_fusion.2
  221.4 2.0 dynamic-slice_bitcast_fusion.2
  224.1 2.0 dynamic-slice_bitcast_fusion.2
  226.8 2.0 dynamic-slice_bitcast_fusion.2
  229.5 2.0 dynamic-slice_bitcast_fusion.2
  232.2 2.0 dynamic-slice_bitcast_fusion.2
  234.9 2.0 dynamic-slice_bitcast_fusion.2
  237.6 2.0 dynamic-slice_bitcast_fusion.2
  763.6 67.5 %reduce-scatter.2.cloned.1.call-done = f32[16,512]{1,0:T(8,128)} async-done(((f32[128,512]{1,0:T(8,128)}), f32[16,512]{1,0:T(8,128)}) %reduce-scatter.2.cloned.1.call-update) | async-done | bytes 32784 | tf_op jit(solution)/shard_map/reduce_scatter | solution.py:62
  (1184 shorter events, 590.9 us)
Async XLA Ops:
  6.5 824.6 %reduce-scatter.2.cloned.1.call-start = ((), (), s32[]{:S(2)}) async-start(), calls=%async_computation.1 | async-start | bytes 294912 | tf_op jit(solution)/shard_map/reduce_scatter | solution.py:62
  7.2 26.4 %collective-permute-start = (bf16[2,3,384]{2,0,1:T(2,128)(2,1)S(1)}, bf16[2,3,384]{2,0,1:T(2,128)(2,1)S(1)}, u32[]{:S(2)}, u32[]{:S(2)}) collective-permute-start(bf16[2,3,384]{2,0,1:T(2,128)(2,1)S(1)} %slice.603), channel_id=1, source_target_pairs={{8,0},{16,8},{24,16},{32,24},{40,32},{48,40},{56,48},{64,56},{72,6... | collective-permute-start | bytes 13832 | tf_op jit(solution)/shard_map/ppermute | solution.py:15
Sparse Core Ops, SparseCore 0:
  763.7 67.3 reduce-scatter.1
where the time goes:
time: 846 us; the launch traced here: 838 us
  local copies, waits for them, and re-layouts  704 us (83%)
  waiting for transfers between devices  67.5 us (8%)
  blocking collectives  20.9 us (2%)
  other arithmetic  20.8 us (2%)
  between operations  14 us (2%)
    gather x1024, local copies, waits for them, and re-layouts  684 us
    reduce_scatter x1, waiting for transfers between devices, local(): lax.psum_scatter(partial_sums, 'sta', scatter_dimension=0, tiled=True)  67.5 us
    all_gather x1, blocking collectives, local(): lax.all_gather(templates, 'tm', axis=0, tiled=True)  20.9 us
    another operation x1, other arithmetic, energy_inverse(): lax.reduce_window(squares, jnp.float32(0.0), lax.add, (1, length), (1, 1)...  19.3 us
    unnamed x204, local copies, waits for them, and re-layouts  18.3 us
  transfers between devices with their start and end apart: 2, of which 1 were waited for; matrix products, arithmetic and copies ran while one was open for 0% of the time, Pallas kernels for 0%

commit v1 on v0

v1 whole, which is shorter than its diff:
```python
import jax
import jax.numpy as jnp
from jax import lax
from jax.experimental import pallas as pl
from jax.experimental.pallas import tpu as pltpu
from jax.sharding import PartitionSpec as P

HALO = 384
EPS = 1e-06
LENGTH = 200
LAG = 64
REACH = 768
SPAN = 896
WIDE = 1024
ROWS = 8
PARTS = LENGTH // LAG + 1


def coordinates(time_index, station_index):
    return time_index // 4, (time_index // 2) % 2, time_index % 2, station_index // 4, station_index % 4


def transposition():
    pairs = []
    for i in range(16):
        for j in range(8):
            x, y, core, high, z = coordinates(i, j)
            target = i // 2
            near, level = target // 4, target % 4
            there = ((x + z - level) % 4) * 4 + (y ^ high ^ near) * 2 + core
            pairs.append((i * 8 + j, there * 8 + target))
    return pairs


def permuted(value, axis, size, move):
    return lax.ppermute(value, axis, [(source, move(source)) for source in range(size)])


def take(value, index):
    return jnp.take_along_axis(value, index, axis=1)


def windows(series, width, steps):
    lane = lax.broadcasted_iota(jnp.int32, (steps.shape[0], 128), 1) + steps
    index, stays = lane & 127, lane < 128
    picked = [take(series[:, at : at + 128], index) for at in range(0, width + 128, 128)]
    return jnp.concatenate([jnp.where(stays, a, b) for a, b in zip(picked[:-1], picked[1:])], axis=1)


def ahead(value, steps):
    return pltpu.roll(value, value.shape[1] - steps, 1)


def kernel(templates_ref, records_ref, out_ref, scale_ref, lagged_ref):
    i, j = lax.axis_index("tm"), lax.axis_index("sta")
    lags = lax.broadcasted_iota(jnp.int32, (LAG, 128), 0)
    energies = []
    for slot in range(8):
        wide = records_ref[slot].astype(jnp.float32)
        squares = wide * wide
        energies.append(squares[0:2] + squares[2:4] + squares[4:6])
        padded = jnp.concatenate([wide, jnp.zeros((ROWS, WIDE - SPAN), jnp.float32)], axis=1)
        for station in range(2):
            for c in range(3):
                row = jnp.broadcast_to(padded[c * 2 + station : c * 2 + station + 1], (LAG, WIDE))
                lagged_ref[slot * 2 + station, c * LAG : (c + 1) * LAG] = windows(row, SPAN, lags).astype(jnp.bfloat16)
    energy = jnp.concatenate(energies, axis=0)
    two = energy + ahead(energy, 1)
    four = two + ahead(two, 2)
    eight = four + ahead(four, 4)
    total, steps = eight, 8
    while steps < 128:
        if steps == 64:
            sixty = total
        total, steps = total + ahead(total, steps), steps * 2
    total = total + ahead(sixty, 128) + ahead(eight, 192)
    scale = lax.rsqrt(total[:, :REACH] + EPS)
    for row in range(16):
        scale_ref[row] = jnp.broadcast_to(scale[row : row + 1], (ROWS, REACH))

    x, y, _, _, z = coordinates(i, j)
    result = jnp.zeros((16, 512), jnp.float32)
    for dx in range(4):
        for dy in range(2):
            slot = lax.rem(x + dx - j // 2 + 8, 4) * 2 + lax.rem(y + dy + j, 2)
            for station in range(2):
                blocks = [templates_ref[dx, dy, core].astype(jnp.float32) for core in range(2)]
                rows = []
                for a in range(PARTS):
                    for block in blocks:
                        pieces = []
                        for c in range(3):
                            top = (station * 3 + c) * ROWS
                            piece = block[top : top + ROWS, a * LAG : (a + 1) * LAG]
                            if (a + 1) * LAG > LENGTH:
                                inside = lax.broadcasted_iota(jnp.int32, (ROWS, LAG), 1) < LENGTH - a * LAG
                                piece = jnp.where(inside, piece, 0.0)
                            pieces.append(piece)
                        rows.append(jnp.concatenate(pieces, axis=1))
                left = jnp.concatenate(rows, axis=0).astype(jnp.bfloat16)
                right = lagged_ref[slot * 2 + station]
                sums = jnp.dot(left, right, preferred_element_type=jnp.float32)
                even = sums[0:16, 0:REACH] + sums[32:48, 128 : 128 + REACH]
                odd = sums[16:32, 0:REACH] + sums[48:64, 128 : 128 + REACH]
                values = even + ahead(odd, LAG)
                values = values * jnp.concatenate([scale_ref[slot * 2 + station]] * 2, axis=0)
                top = station * 3 * ROWS
                moves = jnp.concatenate([block[top : top + ROWS, LENGTH : LENGTH + 1] for block in blocks], axis=0)
                moves = jnp.broadcast_to(moves, (16, 128)).astype(jnp.int32)
                far = moves >= 128
                lane = lax.broadcasted_iota(jnp.int32, (16, 128), 1) + (moves & 127)
                index, stays = lane & 127, lane < 128
                picked = [take(values[:, at : at + 128], index) for at in range(0, REACH, 128)]
                picked = [jnp.where(far, b, a) for a, b in zip(picked[:-1], picked[1:])]
                result += jnp.concatenate([jnp.where(stays, a, b) for a, b in zip(picked[:-1], picked[1:])], axis=1)
    swapped = lax.rem(i, 2) == 1
    low, high = result[0:8], result[8:16]
    out_ref[0:8] = jnp.where(swapped, high, low)
    out_ref[8:16] = jnp.where(swapped, low, high)


def local(records, templates, moveouts):
    i = lax.axis_index("tm")
    mine = lax.dynamic_slice_in_dim(moveouts, i * ROWS, ROWS, 0).astype(jnp.bfloat16)
    mine = jnp.broadcast_to(jnp.transpose(mine)[:, None, :, None], (2, 3, ROWS, 256 - LENGTH))
    packet = jnp.concatenate([jnp.transpose(templates, (1, 2, 0, 3)), mine], axis=3).reshape(6 * ROWS, 256)
    packet = lax.ppermute(packet, ("tm", "sta"), transposition())

    following = lax.ppermute(records[:, :, :HALO], "tm", [(s, s - 1) for s in range(1, 16)])
    extended = jnp.transpose(jnp.concatenate([records, following], axis=2), (1, 0, 2)).reshape(6, SPAN)
    extended = jnp.concatenate([extended, jnp.zeros((2, SPAN), jnp.bfloat16)], axis=0)

    packet = jnp.stack([packet, permuted(packet, "tm", 16, lambda s: s ^ 2)])
    extended = jnp.stack([extended, permuted(extended, "sta", 8, lambda s: s ^ 4)])
    packet = jnp.stack([packet] + [permuted(packet, "tm", 16, lambda s, d=d: (s + 16 - 4 * d) % 16) for d in (1, 2, 3)])
    extended = jnp.stack(
        [extended] + [permuted(extended, "sta", 8, lambda s, d=d: s // 4 * 4 + (s + 4 - d) % 4) for d in (1, 2, 3)]
    )
    packet = jnp.stack([packet, permuted(packet, "tm", 16, lambda s: s ^ 1)], axis=2)

    return pl.pallas_call(
        kernel,
        out_shape=jax.ShapeDtypeStruct((16, 512), jnp.float32),
        in_specs=[pl.BlockSpec(memory_space=pltpu.VMEM)] * 2,
        out_specs=pl.BlockSpec(memory_space=pltpu.VMEM),
        scratch_shapes=[
            pltpu.VMEM((16, ROWS, REACH), jnp.float32),
            pltpu.VMEM((16, 3 * LAG, SPAN), jnp.bfloat16),
        ],
        compiler_params=pltpu.CompilerParams(vmem_limit_bytes=40 * 1024 * 1024),
        cost_estimate=pl.CostEstimate(flops=2 * 128 * 2 * 600 * 696, bytes_accessed=600_000, transcendentals=0),
    )(packet, extended.reshape(8, ROWS, SPAN))


def solution(mesh):
    return jax.shard_map(
        local,
        mesh=mesh,
        in_specs=(P("sta", None, "tm"), P("tm", "sta", None, None), P(None, "sta")),
        out_specs=P("sta", "tm"),
        check_vma=False,
    )
```

time: 846 us -> 43.6 us (0.05)
  the two profiles are of different devices: /device:TPU:1 before, /device:TPU:2 now
where the time goes in v1:
time: 43.6 us; the launch traced here: 43.3 us
  starting transfers between devices  23.6 us (54%)
  waiting for transfers between devices  11.4 us (26%)
  Pallas kernels  7.05 us (16%)
  other arithmetic  0.97 us (2%)
    ppermute x9, starting transfers between devices, permuted(): lax.ppermute(value, axis, [(source, move(source)) for source in range(siz...  14.3 us
    ppermute x9, waiting for transfers between devices, permuted(): lax.ppermute(value, axis, [(source, move(source)) for source in range(siz...  11.4 us
    ppermute x1, starting transfers between devices, local(): packet = lax.ppermute(packet, ('tm', 'sta'), transposition())  7.35 us
    pallas_call x1, Pallas kernels, local(): pl.pallas_call(kernel, out_shape=jax.ShapeDtypeStruct((16, 512), jnp.floa...  7.05 us
    ppermute x1, starting transfers between devices, local(): lax.ppermute(records[:, :, :HALO], 'tm', [(s, s - 1) for s in range(1, 16)])  1.92 us
  transfers between devices with their start and end apart: 11, of which 5 were waited for; matrix products, arithmetic and copies ran while one was open for 0% of the time, Pallas kernels for 0%

profile of v1, /device:TPU:2, one launch (start us, length us, event | category | flops | bytes accessed | tf_op | source)
XLA Modules:
  0.0 43.3 jit_solution(12178336714645796505)
XLA Ops:
  0.0 0.0 copy-start
  0.0 0.8 %fusion = bf16[2,8]{1,0:T(2,128)(2,1)S(1)} fusion(s32[128,2]{0,1:T(2,128)} %param.5, s32[]{:T(128)S(6)} %select_n.3), kind=kLoop, calls=%fused_computation.8 | loop fusion | flops 16 | bytes 100 | tf_op jit(solution)/shard_map/transpose | solution.py:125
  0.8 0.1 copy.4
  0.9 0.1 broadcast_in_dim.2
  0.9 0.0 copy-done
  0.9 0.1 pad_maximum_fusion.5
  1.0 0.0 copy-start.1
  1.1 7.3 %collective-permute-start = (bf16[48,256]{1,0:T(8,128)(2,1)S(1)}, bf16[48,256]{1,0:T(8,128)(2,1)S(1)}, u32[]{:S(2)}, u32[]{:S(2)}) collective-permute-start(bf16[48,256]{1,0:T(8,128)(2,1)S(1)} %bitcast.37), channel_id=1, source_target_pairs={{0,0},{1,32},{2,64},{3,96},{4,16},{5,48},{6,80},{7,112},{8,8},{9,4... | collective-permute-start | bytes 73736 | tf_op jit(solution)/shard_map/ppermute | solution.py:127
  8.4 0.0 copy-done.1
  8.4 1.9 %collective-permute-start.6 = (bf16[2,3,384]{2,0,1:T(2,128)(2,1)S(1)}, bf16[2,3,384]{2,0,1:T(2,128)(2,1)S(1)}, u32[]{:S(2)}, u32[]{:S(2)}) collective-permute-start(bf16[2,3,384]{2,0,1:T(2,128)(2,1)S(1)} %slice.3), channel_id=1, source_target_pairs={{8,0},{16,8},{24,16},{32,24},{40,32},{48,40},{56,48},{64,56},{72,6... | collective-permute-start | bytes 13832 | tf_op jit(solution)/shard_map/ppermute | solution.py:129
  10.4 0.0 collective-permute-done
  10.4 1.3 %collective-permute-start.1 = (bf16[48,256]{1,0:T(8,128)(2,1)S(1)}, bf16[48,256]{1,0:T(8,128)(2,1)S(1)}, u32[]{:S(2)}, u32[]{:S(2)}) collective-permute-start(bf16[48,256]{1,0:T(8,128)(2,1)S(1)} %collective-permute-done), channel_id=1, source_target_pairs={{0,16},{8,24},{16,0},{24,8},{32,48},{40,56},{48,32},{56,40},{64,80... | collective-permute-start | bytes 73736 | tf_op jit(solution)/shard_map/ppermute | solution.py:36
  11.6 0.0 collective-permute-done.6
  11.7 2.6 %collective-permute-done.1 = bf16[48,256]{1,0:T(8,128)(2,1)S(1)} collective-permute-done((bf16[48,256]{1,0:T(8,128)(2,1)S(1)}, bf16[48,256]{1,0:T(8,128)(2,1)S(1)}, u32[]{:S(2)}, u32[]{:S(2)}) %collective-permute-start.1) | collective-permute-done | bytes 24608 | tf_op jit(solution)/shard_map/ppermute | solution.py:36
  14.3 0.1 collective-permute-start.2
  14.4 3.9 %collective-permute-start.3 = (bf16[2,48,256]{2,1,0:T(8,128)(2,1)S(1)}, bf16[2,48,256]{2,1,0:T(8,128)(2,1)S(1)}, u32[]{:S(2)}, u32[]{:S(2)}) collective-permute-start(bf16[2,48,256]{2,1,0:T(8,128)(2,1)S(1)} %get-tuple-element.8), channel_id=1, source_target_pairs={{0,64},{8,72},{16,80},{24,88},{32,96},{40,104},{48,112},{56,120},{... | collective-permute-start | bytes 147464 | tf_op jit(solution)/shard_map/ppermute | solution.py:36
  18.3 2.5 %collective-permute-start.4 = (bf16[2,48,256]{2,1,0:T(8,128)(2,1)S(1)}, bf16[2,48,256]{2,1,0:T(8,128)(2,1)S(1)}, u32[]{:S(2)}, u32[]{:S(2)}) collective-permute-start(bf16[2,48,256]{2,1,0:T(8,128)(2,1)S(1)} %get-tuple-element.8), channel_id=1, source_target_pairs={{0,32},{8,40},{16,48},{24,56},{32,64},{40,72},{48,80},{56,88},{64,... | collective-permute-start | bytes 147464 | tf_op jit(solution)/shard_map/ppermute | solution.py:36
  20.9 0.7 %collective-permute-start.7 = (bf16[8,896]{1,0:T(8,128)(2,1)S(1)}, bf16[8,896]{1,0:T(8,128)(2,1)S(1)}, u32[]{:S(2)}, u32[]{:S(2)}) collective-permute-start(bf16[8,896]{1,0:T(8,128)(2,1)S(1)} %get-tuple-element.12), channel_id=1, source_target_pairs={{0,4},{1,5},{2,6},{3,7},{4,0},{5,1},{6,2},{7,3},{8,12},{9,13},{10,... | collective-permute-start | bytes 43016 | tf_op jit(solution)/shard_map/ppermute | solution.py:36
  21.6 0.0 collective-permute-done.2
  21.6 0.0 collective-permute-done.3
  21.6 1.0 %collective-permute-done.4 = bf16[2,48,256]{2,1,0:T(8,128)(2,1)S(1)} collective-permute-done((bf16[2,48,256]{2,1,0:T(8,128)(2,1)S(1)}, bf16[2,48,256]{2,1,0:T(8,128)(2,1)S(1)}, u32[]{:S(2)}, u32[]{:S(2)}) %collective-permute-start.4) | collective-permute-done | bytes 49184 | tf_op jit(solution)/shard_map/ppermute | solution.py:36
  22.7 0.1 collective-permute-start.5
  22.7 3.3 %collective-permute-done.7 = bf16[8,896]{1,0:T(8,128)(2,1)S(1)} collective-permute-done((bf16[8,896]{1,0:T(8,128)(2,1)S(1)}, bf16[8,896]{1,0:T(8,128)(2,1)S(1)}, u32[]{:S(2)}, u32[]{:S(2)}) %collective-permute-start.7) | collective-permute-done | bytes 14368 | tf_op jit(solution)/shard_map/ppermute | solution.py:36
  26.1 4.7 %collective-permute-start.8 = (bf16[2,8,896]{2,1,0:T(8,128)(2,1)S(1)}, bf16[2,8,896]{2,1,0:T(8,128)(2,1)S(1)}, u32[]{:S(2)}, u32[]{:S(2)}) collective-permute-start(bf16[2,8,896]{2,1,0:T(8,128)(2,1)S(1)} %get-tuple-element.10), channel_id=1, source_target_pairs={{0,3},{1,0},{2,1},{3,2},{4,7},{5,4},{6,5},{7,6},{8,11},{9,8},{10,9... | collective-permute-start | bytes 86024 | tf_op jit(solution)/shard_map/ppermute | solution.py:36
  30.8 0.0 collective-permute-start.9
  30.8 0.9 %collective-permute-start.10 = (bf16[2,8,896]{2,1,0:T(8,128)(2,1)S(1)}, bf16[2,8,896]{2,1,0:T(8,128)(2,1)S(1)}, u32[]{:S(2)}, u32[]{:S(2)}) collective-permute-start(bf16[2,8,896]{2,1,0:T(8,128)(2,1)S(1)} %get-tuple-element.10), channel_id=1, source_target_pairs={{0,1},{1,2},{2,3},{3,0},{4,5},{5,6},{6,7},{7,4},{8,9},{9,10},{10,1... | collective-permute-start | bytes 86024 | tf_op jit(solution)/shard_map/ppermute | solution.py:36
  31.8 0.6 %collective-permute-done.8 = bf16[2,8,896]{2,1,0:T(8,128)(2,1)S(1)} collective-permute-done((bf16[2,8,896]{2,1,0:T(8,128)(2,1)S(1)}, bf16[2,8,896]{2,1,0:T(8,128)(2,1)S(1)}, u32[]{:S(2)}, u32[]{:S(2)}) %collective-permute-start.8) | collective-permute-done | bytes 28704 | tf_op jit(solution)/shard_map/ppermute | solution.py:36
  32.4 3.8 %collective-permute-done.9 = bf16[2,8,896]{2,1,0:T(8,128)(2,1)S(1)} collective-permute-done((bf16[2,8,896]{2,1,0:T(8,128)(2,1)S(1)}, bf16[2,8,896]{2,1,0:T(8,128)(2,1)S(1)}, u32[]{:S(2)}, u32[]{:S(2)}) %collective-permute-start.9) | collective-permute-done | bytes 28704 | tf_op jit(solution)/shard_map/ppermute | solution.py:36
  36.2 0.0 collective-permute-done.10
  36.2 0.0 collective-permute-done.5
  36.3 7.1 %shard_map.37 = f32[16,512]{1,0:T(8,128)} custom-call(bf16[4,2,2,48,256]{4,3,2,1,0:T(8,128)(2,1)S(1)} %pad_maximum_fusion.templates_ref, bf16[8,8,896]{2,1,0:T(8,128)(2,1)S(1)} %bitcast.27), custom_call_target="tpu_custom_call" | custom-call | flops 213811200 | bytes 600000 | tf_op jit(solution)/shard_map/pallas_call | solution.py:141
  (10 shorter events, 0.2 us)
Async XLA Ops:
  0.0 0.9 %copy-start = (bf16[8,2,3,200]{3,1,2,0:T(2,128)(2,1)S(1)}, bf16[8,2,3,200]{3,1,2,0:T(2,128)(2,1)}, u32[]{:S(2)}) copy-start(bf16[8,2,3,200]{3,1,2,0:T(2,128)(2,1)} %param.4) | copy-start | bytes 57604
  1.0 7.4 %copy-start.1 = (bf16[2,3,512]{2,0,1:T(2,128)(2,1)S(1)}, bf16[2,3,512]{2,0,1:T(2,128)(2,1)}, u32[]{:S(2)}) copy-start(bf16[2,3,512]{2,0,1:T(2,128)(2,1)} %param.3) | copy-start | bytes 18436
  1.1 9.3 %collective-permute-start = (bf16[48,256]{1,0:T(8,128)(2,1)S(1)}, bf16[48,256]{1,0:T(8,128)(2,1)S(1)}, u32[]{:S(2)}, u32[]{:S(2)}) collective-permute-start(bf16[48,256]{1,0:T(8,128)(2,1)S(1)} %bitcast.37), channel_id=1, source_target_pairs={{0,0},{1,32},{2,64},{3,96},{4,16},{5,48},{6,80},{7,112},{8,8},{9,4... | collective-permute-start | bytes 73736 | tf_op jit(solution)/shard_map/ppermute | solution.py:127
  8.4 3.2 %collective-permute-start.6 = (bf16[2,3,384]{2,0,1:T(2,128)(2,1)S(1)}, bf16[2,3,384]{2,0,1:T(2,128)(2,1)S(1)}, u32[]{:S(2)}, u32[]{:S(2)}) collective-permute-start(bf16[2,3,384]{2,0,1:T(2,128)(2,1)S(1)} %slice.3), channel_id=1, source_target_pairs={{8,0},{16,8},{24,16},{32,24},{40,32},{48,40},{56,48},{64,56},{72,6... | collective-permute-start | bytes 13832 | tf_op jit(solution)/shard_map/ppermute | solution.py:129
  10.4 3.9 %collective-permute-start.1 = (bf16[48,256]{1,0:T(8,128)(2,1)S(1)}, bf16[48,256]{1,0:T(8,128)(2,1)S(1)}, u32[]{:S(2)}, u32[]{:S(2)}) collective-permute-start(bf16[48,256]{1,0:T(8,128)(2,1)S(1)} %collective-permute-done), channel_id=1, source_target_pairs={{0,16},{8,24},{16,0},{24,8},{32,48},{40,56},{48,32},{56,40},{64,80... | collective-permute-start | bytes 73736 | tf_op jit(solution)/shard_map/ppermute | solution.py:36
  14.3 7.3 %collective-permute-start.2 = (bf16[2,48,256]{2,1,0:T(8,128)(2,1)S(1)}, bf16[2,48,256]{2,1,0:T(8,128)(2,1)S(1)}, u32[]{:S(2)}, u32[]{:S(2)}) collective-permute-start(bf16[2,48,256]{2,1,0:T(8,128)(2,1)S(1)} %get-tuple-element.8), channel_id=1, source_target_pairs={{0,96},{8,104},{16,112},{24,120},{32,0},{40,8},{48,16},{56,24},{64... | collective-permute-start | bytes 147464 | tf_op jit(solution)/shard_map/ppermute | solution.py:36
  14.4 7.2 %collective-permute-start.3 = (bf16[2,48,256]{2,1,0:T(8,128)(2,1)S(1)}, bf16[2,48,256]{2,1,0:T(8,128)(2,1)S(1)}, u32[]{:S(2)}, u32[]{:S(2)}) collective-permute-start(bf16[2,48,256]{2,1,0:T(8,128)(2,1)S(1)} %get-tuple-element.8), channel_id=1, source_target_pairs={{0,64},{8,72},{16,80},{24,88},{32,96},{40,104},{48,112},{56,120},{... | collective-permute-start | bytes 147464 | tf_op jit(solution)/shard_map/ppermute | solution.py:36
  18.3 4.3 %collective-permute-start.4 = (bf16[2,48,256]{2,1,0:T(8,128)(2,1)S(1)}, bf16[2,48,256]{2,1,0:T(8,128)(2,1)S(1)}, u32[]{:S(2)}, u32[]{:S(2)}) collective-permute-start(bf16[2,48,256]{2,1,0:T(8,128)(2,1)S(1)} %get-tuple-element.8), channel_id=1, source_target_pairs={{0,32},{8,40},{16,48},{24,56},{32,64},{40,72},{48,80},{56,88},{64,... | collective-permute-start | bytes 147464 | tf_op jit(solution)/shard_map/ppermute | solution.py:36
  20.9 5.2 %collective-permute-start.7 = (bf16[8,896]{1,0:T(8,128)(2,1)S(1)}, bf16[8,896]{1,0:T(8,128)(2,1)S(1)}, u32[]{:S(2)}, u32[]{:S(2)}) collective-permute-start(bf16[8,896]{1,0:T(8,128)(2,1)S(1)} %get-tuple-element.12), channel_id=1, source_target_pairs={{0,4},{1,5},{2,6},{3,7},{4,0},{5,1},{6,2},{7,3},{8,12},{9,13},{10,... | collective-permute-start | bytes 43016 | tf_op jit(solution)/shard_map/ppermute | solution.py:36
  22.7 13.6 %collective-permute-start.5 = (bf16[4,2,48,256]{3,2,1,0:T(8,128)(2,1)S(1)}, bf16[4,2,48,256]{3,2,1,0:T(8,128)(2,1)S(1)}, u32[]{:S(2)}, u32[]{:S(2)}) collective-permute-start(bf16[4,2,48,256]{3,2,1,0:T(8,128)(2,1)S(1)} %get-tuple-element.6), channel_id=1, source_target_pairs={{0,8},{8,0},{16,24},{24,16},{32,40},{40,32},{48,56},{56,48},{64,72... | collective-permute-start | bytes 589832 | tf_op jit(solution)/shard_map/ppermute | solution.py:36
  26.1 6.3 %collective-permute-start.8 = (bf16[2,8,896]{2,1,0:T(8,128)(2,1)S(1)}, bf16[2,8,896]{2,1,0:T(8,128)(2,1)S(1)}, u32[]{:S(2)}, u32[]{:S(2)}) collective-permute-start(bf16[2,8,896]{2,1,0:T(8,128)(2,1)S(1)} %get-tuple-element.10), channel_id=1, source_target_pairs={{0,3},{1,0},{2,1},{3,2},{4,7},{5,4},{6,5},{7,6},{8,11},{9,8},{10,9... | collective-permute-start | bytes 86024 | tf_op jit(solution)/shard_map/ppermute | solution.py:36
  30.8 5.4 %collective-permute-start.9 = (bf16[2,8,896]{2,1,0:T(8,128)(2,1)S(1)}, bf16[2,8,896]{2,1,0:T(8,128)(2,1)S(1)}, u32[]{:S(2)}, u32[]{:S(2)}) collective-permute-start(bf16[2,8,896]{2,1,0:T(8,128)(2,1)S(1)} %get-tuple-element.10), channel_id=1, source_target_pairs={{0,2},{1,3},{2,0},{3,1},{4,6},{5,7},{6,4},{7,5},{8,10},{9,11},{10,... | collective-permute-start | bytes 86024 | tf_op jit(solution)/shard_map/ppermute | solution.py:36
  30.8 5.4 %collective-permute-start.10 = (bf16[2,8,896]{2,1,0:T(8,128)(2,1)S(1)}, bf16[2,8,896]{2,1,0:T(8,128)(2,1)S(1)}, u32[]{:S(2)}, u32[]{:S(2)}) collective-permute-start(bf16[2,8,896]{2,1,0:T(8,128)(2,1)S(1)} %get-tuple-element.10), channel_id=1, source_target_pairs={{0,1},{1,2},{2,3},{3,0},{4,5},{5,6},{6,7},{7,4},{8,9},{9,10},{10,1... | collective-permute-start | bytes 86024 | tf_op jit(solution)/shard_map/ppermute | solution.py:36

commit v2 on v1

v2 whole, which is shorter than its diff:
```python
import jax
import jax.numpy as jnp
from jax import lax
from jax.experimental import pallas as pl
from jax.experimental.pallas import tpu as pltpu
from jax.sharding import PartitionSpec as P

EPS = 1e-06
LENGTH = 200
LAG = 64
REACH = 768
SPAN = 896
BLOCK = 6 * 8
WIDE = 1024
ROWS = 8
SENDER = 1
PARTS = LENGTH // LAG + 1


def coordinates(time_index, station_index):
    return time_index // 4, (time_index // 2) % 2, time_index % 2, station_index // 4, station_index % 4


def exchange(value, templates_to, records_to):
    pairs = []
    for i in range(16):
        for j in range(8):
            target = (templates_to if i % 2 == SENDER else records_to)(*coordinates(i, j))
            if target is not None:
                x, y, core, high, z = target
                pairs.append((i * 8 + j, ((x * 2 + y) * 2 + core) * 8 + high * 4 + z))
    return lax.ppermute(value, ("tm", "sta"), pairs)


def other_core(x, y, core, high, z):
    return x, y, 1 - core, high, z


def to_owner(x, y, core, high, z):
    near, level = x // 2, x % 2 * 2 + y
    return (x + 2 + z - level) % 4, y ^ high ^ near, core, near, level


def to_previous(x, y, core, high, z):
    return None if x + y == 0 else (x - 1 + y, 1 - y, core, high, z)


def across_y(x, y, core, high, z):
    return x, 1 - y, core, high, z


def across_high(x, y, core, high, z):
    return x, y, core, 1 - high, z


def back_x(steps):
    return lambda x, y, core, high, z: ((x - steps) % 4, y, core, high, z)


def back_z(steps):
    return lambda x, y, core, high, z: (x, y, core, high, (z - steps) % 4)


def take(value, index):
    return jnp.take_along_axis(value, index, axis=1)


def windows(series):
    return pltpu.roll(series, WIDE - LAG + 1, 1, stride=1, stride_axis=0)[:, :SPAN].astype(jnp.bfloat16)


def ahead(value, steps):
    return pltpu.roll(value, value.shape[1] - steps, 1)


def kernel(gathered_ref, out_ref, scale_ref, lagged_ref, flipped_ref, moves_ref):
    i, j = lax.axis_index("tm"), lax.axis_index("sta")
    x, y, core, _, z = coordinates(i, j)
    sender = jnp.where(core == SENDER, 0, 1)
    energies = []
    for slot in range(8):
        rows = pl.ds(pl.multiple_of(core * 16, 16), 32)
        chunks = gathered_ref[1 - sender, slot // 2, slot % 2, 0, rows].astype(jnp.float32)
        wide = jnp.concatenate([chunks[at * ROWS : (at + 1) * ROWS] for at in range(4)], axis=1)
        squares = wide * wide
        energies.append(squares[0:2] + squares[2:4] + squares[4:6])
        for station in range(2):
            for c in range(3):
                row = jnp.broadcast_to(wide[c * 2 + station : c * 2 + station + 1], (LAG, WIDE))
                lagged_ref[slot * 2 + station, c * LAG : (c + 1) * LAG] = windows(row)
    energy = jnp.concatenate(energies, axis=0)
    two = energy + ahead(energy, 1)
    four = two + ahead(two, 2)
    eight = four + ahead(four, 4)
    total, steps = eight, 8
    while steps < 128:
        if steps == 64:
            sixty = total
        total, steps = total + ahead(total, steps), steps * 2
    total = total + ahead(sixty, 128) + ahead(eight, 192)
    scale = lax.rsqrt(total[:, :REACH] + EPS)
    for row in range(16):
        scale_ref[row] = jnp.broadcast_to(scale[row : row + 1], (ROWS, REACH))

    blocks = gathered_ref[sender].reshape(16 * BLOCK, 256)
    source = lax.broadcasted_iota(jnp.int32, (256, 256), 0)
    target = lax.broadcasted_iota(jnp.int32, (256, 256), 1)
    flip = jnp.where((source < LENGTH) & (source == (target ^ (LAG - 1))), 1.0, 0.0).astype(jnp.bfloat16)
    flipped_ref[...] = jnp.dot(blocks, flip, preferred_element_type=jnp.float32)
    spread = jnp.where(source[:, :128] == LENGTH, 1.0, 0.0).astype(jnp.bfloat16)
    moves_ref[...] = jnp.dot(blocks, spread, preferred_element_type=jnp.float32).astype(jnp.int32)

    lane = lax.broadcasted_iota(jnp.int32, (16, 128), 1)
    result = jnp.zeros((16, 512), jnp.float32)
    for dx in range(4):
        for dy in range(2):
            slot = lax.rem(x + dx - j // 2 + 6, 4) * 2 + lax.rem(y + dy + j, 2)
            for station in range(2):
                tops = [((dx * 2 + dy) * 2 + half) * BLOCK + station * 3 * ROWS for half in range(2)]
                rows = []
                for a in range(PARTS):
                    for top in tops:
                        pieces = [
                            flipped_ref[top + c * ROWS : top + (c + 1) * ROWS, a * LAG : (a + 1) * LAG] for c in range(3)
                        ]
                        rows.append(jnp.concatenate(pieces, axis=1))
                left = jnp.concatenate(rows, axis=0).astype(jnp.bfloat16)
                right = lagged_ref[slot * 2 + station]
                sums = jnp.dot(left, right, preferred_element_type=jnp.float32)
                even = sums[0:16, 0:REACH] + sums[32:48, 128 : 128 + REACH]
                odd = sums[16:32, 0:REACH] + sums[48:64, 128 : 128 + REACH]
                values = even + ahead(odd, LAG)
                values = values * jnp.concatenate([scale_ref[slot * 2 + station]] * 2, axis=0)
                moves = jnp.concatenate([moves_ref[top : top + ROWS] for top in tops], axis=0)
                near = moves & 127
                picked = [values[:, at : at + 128] for at in range(0, REACH, 128)]
                picked = [jnp.where(moves >= 128, b, a) for a, b in zip(picked[:-1], picked[1:])]
                picked = [jnp.where(lane < near, b, a) for a, b in zip(picked[:-1], picked[1:])]
                index = (lane + near) & 127
                result += jnp.concatenate([take(value, index) for value in picked], axis=1)
    out_ref[...] = result


def local(records, templates, moveouts):
    i = lax.axis_index("tm")
    mine = lax.dynamic_slice_in_dim(moveouts, i * ROWS, ROWS, 0).astype(jnp.bfloat16)
    mine = jnp.broadcast_to(jnp.transpose(mine)[:, None, :, None], (2, 3, ROWS, 256 - LENGTH))
    packet = jnp.concatenate([jnp.transpose(templates, (1, 2, 0, 3)), mine], axis=3).reshape(6 * ROWS, 256)
    series = jnp.transpose(records, (1, 0, 2)).reshape(6, 512)
    series = jnp.concatenate([series, jnp.zeros((2, 512), jnp.bfloat16)], axis=0)
    series = jnp.concatenate([series[:, :256], series[:, 256:]], axis=0)

    first = i % 2 == SENDER
    spare = jnp.zeros((BLOCK, 256), jnp.bfloat16)
    series = jnp.concatenate([series, spare[16:]], axis=0)
    came = exchange(jnp.where(first, series, packet), other_core, other_core)
    mine = jnp.where(first, packet, series)
    next_came = exchange(jnp.concatenate([jnp.where(first, came, mine), mine], axis=0), to_owner, to_previous)
    chip_series = jnp.concatenate([mine[:16], came[:16], next_came[:16], spare], axis=0)
    held = jnp.where(first, next_came, chip_series)
    held = jnp.stack([held, exchange(held, across_y, across_high)])
    held = jnp.stack([held] + [exchange(held, back_x(steps), back_z(steps)) for steps in (1, 2, 3)])
    held = jnp.stack([held, exchange(held, other_core, other_core)])

    return pl.pallas_call(
        kernel,
        out_shape=jax.ShapeDtypeStruct((16, 512), jnp.float32),
        in_specs=[pl.BlockSpec(memory_space=pltpu.VMEM)],
        out_specs=pl.BlockSpec(memory_space=pltpu.VMEM),
        scratch_shapes=[
            pltpu.VMEM((16, ROWS, REACH), jnp.float32),
            pltpu.VMEM((16, 3 * LAG, SPAN), jnp.bfloat16),
            pltpu.VMEM((16 * BLOCK, 256), jnp.float32),
            pltpu.VMEM((16 * BLOCK, 128), jnp.int32),
        ],
        compiler_params=pltpu.CompilerParams(vmem_limit_bytes=40 * 1024 * 1024),
        cost_estimate=pl.CostEstimate(flops=2 * 128 * 2 * 600 * 696, bytes_accessed=600_000, transcendentals=0),
    )(held.reshape(2, 4, 2, 2, BLOCK, 256))


def solution(mesh):
    return jax.shard_map(
        local,
        mesh=mesh,
        in_specs=(P("sta", None, "tm"), P("tm", "sta", None, None), P(None, "sta")),
        out_specs=P("sta", "tm"),
        check_vma=False,
    )
```

time: 43.6 us -> 33.3 us (0.76)
  the two profiles are of different devices: /device:TPU:2 before, /device:TPU:1 now
where the time goes in v2:
time: 33.3 us; the launch traced here: 32.8 us
  starting transfers between devices  16.2 us (49%)
  waiting for transfers between devices  9.66 us (29%)
  Pallas kernels  4.66 us (14%)
  local copies, waits for them, and re-layouts  1.68 us (5%)
  other arithmetic  0.56 us (2%)
    ppermute x7, starting transfers between devices, exchange(): return lax.ppermute(value, ('tm', 'sta'), pairs)  16.2 us
    ppermute x7, waiting for transfers between devices, exchange(): return lax.ppermute(value, ('tm', 'sta'), pairs)  9.66 us
    pallas_call x1, Pallas kernels, local(): pl.pallas_call(kernel, out_shape=jax.ShapeDtypeStruct((16, 512), jnp.floa...  4.66 us
    unnamed x9, local copies, waits for them, and re-layouts  1.42 us
  transfers between devices with their start and end apart: 7, of which 7 were waited for; matrix products, arithmetic and copies ran while one was open for 0% of the time, Pallas kernels for 0%

profile of v2, /device:TPU:1, one launch (start us, length us, event | category | flops | bytes accessed | tf_op | source)
XLA Modules:
  0.0 32.8 jit_solution(14249700198761358019)
XLA Ops:
  0.0 0.0 copy-start.2
  0.0 0.0 copy-start.1
  0.0 0.7 %copy-done.2 = bf16[2,3,512]{2,0,1:T(2,128)(2,1)S(1)} copy-done((bf16[2,3,512]{2,0,1:T(2,128)(2,1)S(1)}, bf16[2,3,512]{2,0,1:T(2,128)(2,1)}, u32[]{:S(2)}) %copy-start.2) | copy-done | bytes 6168
  0.7 0.0 copy-done.1
  0.8 0.0 copy-start.3
  0.8 0.7 %copy-done.3 = s32[128,2]{0,1:T(2,128)S(1)} copy-done((s32[128,2]{0,1:T(2,128)S(1)}, s32[128,2]{0,1:T(2,128)}, u32[]{:S(2)}) %copy-start.3) | copy-done | bytes 1048
  1.4 0.1 fusion
  1.5 0.1 pad.23.clone
  1.6 0.1 broadcast_in_dim.4
  1.7 0.1 pad_maximum_fusion.4
  1.8 0.1 bitcast_select_fusion.1
  1.8 1.4 %collective-permute-start = (bf16[48,256]{1,0:T(8,128)(2,1)S(1)}, bf16[48,256]{1,0:T(8,128)(2,1)S(1)}, u32[]{:S(2)}, u32[]{:S(2)}) collective-permute-start(bf16[48,256]{1,0:T(8,128)(2,1)S(1)} %bitcast_select_fusion.1), channel_id=1, source_target_pairs={{0,8},{1,9},{2,10},{3,11},{4,12},{5,13},{6,14},{7,15},{8,0},{9,1},... | collective-permute-start | bytes 73736 | tf_op jit(solution)/shard_map/ppermute | solution.py:32
  3.3 0.8 %collective-permute-done = bf16[48,256]{1,0:T(8,128)(2,1)S(1)} collective-permute-done((bf16[48,256]{1,0:T(8,128)(2,1)S(1)}, bf16[48,256]{1,0:T(8,128)(2,1)S(1)}, u32[]{:S(2)}, u32[]{:S(2)}) %collective-permute-start) | collective-permute-done | bytes 24608 | tf_op jit(solution)/shard_map/ppermute | solution.py:32
  4.1 0.0 copy-start
  4.1 0.1 broadcast_select_fusion
  4.2 4.7 %collective-permute-start.1 = (bf16[96,256]{1,0:T(8,128)(2,1)S(1)}, bf16[96,256]{1,0:T(8,128)(2,1)S(1)}, u32[]{:S(2)}, u32[]{:S(2)}) collective-permute-start(bf16[96,256]{1,0:T(8,128)(2,1)S(1)} %pad_maximum_fusion.3), channel_id=1, source_target_pairs={{8,72},{9,104},{10,8},{11,40},{12,88},{13,120},{14,24},{15,56},{16... | collective-permute-start | bytes 147464 | tf_op jit(solution)/shard_map/ppermute | solution.py:32
  9.0 0.1 pad.16.clone
  9.0 0.0 copy-done
  9.0 0.0 slice-start
  9.1 2.2 %collective-permute-done.1 = bf16[96,256]{1,0:T(8,128)(2,1)S(1)} collective-permute-done((bf16[96,256]{1,0:T(8,128)(2,1)S(1)}, bf16[96,256]{1,0:T(8,128)(2,1)S(1)}, u32[]{:S(2)}, u32[]{:S(2)}) %collective-permute-start.1) | collective-permute-done | bytes 49184 | tf_op jit(solution)/shard_map/ppermute | solution.py:32
  11.3 0.0 slice-done
  11.3 0.1 maximum_select_fusion
  11.4 2.4 %collective-permute-start.2 = (bf16[96,256]{1,0:T(8,128)(2,1)S(1)}, bf16[96,256]{1,0:T(8,128)(2,1)S(1)}, u32[]{:S(2)}, u32[]{:S(2)}) collective-permute-start(bf16[96,256]{1,0:T(8,128)(2,1)S(1)} %maximum_select_fusion), channel_id=1, source_target_pairs={{0,4},{1,5},{2,6},{3,7},{4,0},{5,1},{6,2},{7,3},{8,24},{9,25},{10,... | collective-permute-start | bytes 147464 | tf_op jit(solution)/shard_map/ppermute | solution.py:32
  13.8 1.8 %collective-permute-done.2 = bf16[96,256]{1,0:T(8,128)(2,1)S(1)} collective-permute-done((bf16[96,256]{1,0:T(8,128)(2,1)S(1)}, bf16[96,256]{1,0:T(8,128)(2,1)S(1)}, u32[]{:S(2)}, u32[]{:S(2)}) %collective-permute-start.2) | collective-permute-done | bytes 49184 | tf_op jit(solution)/shard_map/ppermute | solution.py:32
  15.5 1.4 %collective-permute-start.5 = (bf16[2,96,256]{2,1,0:T(8,128)(2,1)S(1)}, bf16[2,96,256]{2,1,0:T(8,128)(2,1)S(1)}, u32[]{:S(2)}, u32[]{:S(2)}) collective-permute-start(bf16[2,96,256]{2,1,0:T(8,128)(2,1)S(1)} %get-tuple-element.8), channel_id=1, source_target_pairs={{0,1},{1,2},{2,3},{3,0},{4,5},{5,6},{6,7},{7,4},{8,40},{9,41},{10,... | collective-permute-start | bytes 294920 | tf_op jit(solution)/shard_map/ppermute | solution.py:32
  17.0 3.3 %collective-permute-start.4 = (bf16[2,96,256]{2,1,0:T(8,128)(2,1)S(1)}, bf16[2,96,256]{2,1,0:T(8,128)(2,1)S(1)}, u32[]{:S(2)}, u32[]{:S(2)}) collective-permute-start(bf16[2,96,256]{2,1,0:T(8,128)(2,1)S(1)} %get-tuple-element.8), channel_id=1, source_target_pairs={{0,2},{1,3},{2,0},{3,1},{4,6},{5,7},{6,4},{7,5},{8,72},{9,73},{10,... | collective-permute-start | bytes 294920 | tf_op jit(solution)/shard_map/ppermute | solution.py:32
  20.3 0.0 collective-permute-start.3
  20.3 0.8 %collective-permute-done.5 = bf16[2,96,256]{2,1,0:T(8,128)(2,1)S(1)} collective-permute-done((bf16[2,96,256]{2,1,0:T(8,128)(2,1)S(1)}, bf16[2,96,256]{2,1,0:T(8,128)(2,1)S(1)}, u32[]{:S(2)}, u32[]{:S(2)}) %collective-permute-start.5) | collective-permute-done | bytes 98336 | tf_op jit(solution)/shard_map/ppermute | solution.py:32
  21.1 2.2 %collective-permute-done.4 = bf16[2,96,256]{2,1,0:T(8,128)(2,1)S(1)} collective-permute-done((bf16[2,96,256]{2,1,0:T(8,128)(2,1)S(1)}, bf16[2,96,256]{2,1,0:T(8,128)(2,1)S(1)}, u32[]{:S(2)}, u32[]{:S(2)}) %collective-permute-start.4) | collective-permute-done | bytes 98336 | tf_op jit(solution)/shard_map/ppermute | solution.py:32
  23.3 0.4 %collective-permute-done.3 = bf16[2,96,256]{2,1,0:T(8,128)(2,1)S(1)} collective-permute-done((bf16[2,96,256]{2,1,0:T(8,128)(2,1)S(1)}, bf16[2,96,256]{2,1,0:T(8,128)(2,1)S(1)}, u32[]{:S(2)}, u32[]{:S(2)}) %collective-permute-start.3) | collective-permute-done | bytes 98336 | tf_op jit(solution)/shard_map/ppermute | solution.py:32
  23.7 0.1 pad_maximum_fusion.1
  23.8 2.9 %collective-permute-start.6 = (bf16[4,2,96,256]{3,2,1,0:T(8,128)(2,1)S(1)}, bf16[4,2,96,256]{3,2,1,0:T(8,128)(2,1)S(1)}, u32[]{:S(2)}, u32[]{:S(2)}) collective-permute-start(bf16[4,2,96,256]{3,2,1,0:T(8,128)(2,1)S(1)} %pad_maximum_fusion.1), channel_id=1, source_target_pairs={{0,8},{1,9},{2,10},{3,11},{4,12},{5,13},{6,14},{7,15},{8,0},{9,1},... | collective-permute-start | bytes 1179656 | tf_op jit(solution)/shard_map/ppermute | solution.py:32
  26.7 1.3 %collective-permute-done.6 = bf16[4,2,96,256]{3,2,1,0:T(8,128)(2,1)S(1)} collective-permute-done((bf16[4,2,96,256]{3,2,1,0:T(8,128)(2,1)S(1)}, bf16[4,2,96,256]{3,2,1,0:T(8,128)(2,1)S(1)}, u32[]{:S(2)}, u32[]{:S(2)}) %collective-permute-start.6) | collective-permute-done | bytes 393248 | tf_op jit(solution)/shard_map/ppermute | solution.py:32
  28.1 0.1 pad_maximum_fusion.gathered_ref
  28.2 4.7 %shard_map.37 = f32[16,512]{1,0:T(8,128)} custom-call(bf16[2,4,2,2,48,256]{5,4,3,2,1,0:T(8,128)(2,1)S(1)} %pad_maximum_fusion.gathered_ref), custom_call_target="tpu_custom_call" | custom-call | flops 213811200 | bytes 600000 | tf_op jit(solution)/shard_map/pallas_call | solution.py:165
  (9 shorter events, 0.1 us)
Async XLA Ops:
  0.0 0.7 %copy-start.2 = (bf16[2,3,512]{2,0,1:T(2,128)(2,1)S(1)}, bf16[2,3,512]{2,0,1:T(2,128)(2,1)}, u32[]{:S(2)}) copy-start(bf16[2,3,512]{2,0,1:T(2,128)(2,1)} %param.3) | copy-start | bytes 18436
  0.0 0.8 %copy-start.1 = (bf16[8,2,3,200]{3,1,2,0:T(2,128)(2,1)S(1)}, bf16[8,2,3,200]{3,1,2,0:T(2,128)(2,1)}, u32[]{:S(2)}) copy-start(bf16[8,2,3,200]{3,1,2,0:T(2,128)(2,1)} %param.4) | copy-start | bytes 57604
  0.8 0.7 %copy-start.3 = (s32[128,2]{0,1:T(2,128)S(1)}, s32[128,2]{0,1:T(2,128)}, u32[]{:S(2)}) copy-start(s32[128,2]{0,1:T(2,128)} %param.5) | copy-start | bytes 3076
  1.8 2.3 %collective-permute-start = (bf16[48,256]{1,0:T(8,128)(2,1)S(1)}, bf16[48,256]{1,0:T(8,128)(2,1)S(1)}, u32[]{:S(2)}, u32[]{:S(2)}) collective-permute-start(bf16[48,256]{1,0:T(8,128)(2,1)S(1)} %bitcast_select_fusion.1), channel_id=1, source_target_pairs={{0,8},{1,9},{2,10},{3,11},{4,12},{5,13},{6,14},{7,15},{8,0},{9,1},... | collective-permute-start | bytes 73736 | tf_op jit(solution)/shard_map/ppermute | solution.py:32
  4.1 4.9 %copy-start = (bf16[48,256]{1,0:T(8,128)(2,1)}, bf16[48,256]{1,0:T(8,128)(2,1)S(1)}, u32[]{:S(2)}) copy-start(bf16[48,256]{1,0:T(8,128)(2,1)S(1)} %collective-permute-done) | copy-start | bytes 73732
  4.2 7.1 %collective-permute-start.1 = (bf16[96,256]{1,0:T(8,128)(2,1)S(1)}, bf16[96,256]{1,0:T(8,128)(2,1)S(1)}, u32[]{:S(2)}, u32[]{:S(2)}) collective-permute-start(bf16[96,256]{1,0:T(8,128)(2,1)S(1)} %pad_maximum_fusion.3), channel_id=1, source_target_pairs={{8,72},{9,104},{10,8},{11,40},{12,88},{13,120},{14,24},{15,56},{16... | collective-permute-start | bytes 147464 | tf_op jit(solution)/shard_map/ppermute | solution.py:32
  9.0 2.2 %slice-start = ((bf16[48,256]{1,0:T(8,128)(2,1)}), bf16[16,256]{1,0:T(8,128)(2,1)S(1)}, s32[]{:S(2)}) async-start(bf16[48,256]{1,0:T(8,128)(2,1)} %copy-done), calls=%async_computation | async-start | bytes 16384 | tf_op jit(solution)/shard_map/slice | solution.py:159
  11.4 4.2 %collective-permute-start.2 = (bf16[96,256]{1,0:T(8,128)(2,1)S(1)}, bf16[96,256]{1,0:T(8,128)(2,1)S(1)}, u32[]{:S(2)}, u32[]{:S(2)}) collective-permute-start(bf16[96,256]{1,0:T(8,128)(2,1)S(1)} %maximum_select_fusion), channel_id=1, source_target_pairs={{0,4},{1,5},{2,6},{3,7},{4,0},{5,1},{6,2},{7,3},{8,24},{9,25},{10,... | collective-permute-start | bytes 147464 | tf_op jit(solution)/shard_map/ppermute | solution.py:32
  15.5 5.6 %collective-permute-start.5 = (bf16[2,96,256]{2,1,0:T(8,128)(2,1)S(1)}, bf16[2,96,256]{2,1,0:T(8,128)(2,1)S(1)}, u32[]{:S(2)}, u32[]{:S(2)}) collective-permute-start(bf16[2,96,256]{2,1,0:T(8,128)(2,1)S(1)} %get-tuple-element.8), channel_id=1, source_target_pairs={{0,1},{1,2},{2,3},{3,0},{4,5},{5,6},{6,7},{7,4},{8,40},{9,41},{10,... | collective-permute-start | bytes 294920 | tf_op jit(solution)/shard_map/ppermute | solution.py:32
  17.0 6.4 %collective-permute-start.4 = (bf16[2,96,256]{2,1,0:T(8,128)(2,1)S(1)}, bf16[2,96,256]{2,1,0:T(8,128)(2,1)S(1)}, u32[]{:S(2)}, u32[]{:S(2)}) collective-permute-start(bf16[2,96,256]{2,1,0:T(8,128)(2,1)S(1)} %get-tuple-element.8), channel_id=1, source_target_pairs={{0,2},{1,3},{2,0},{3,1},{4,6},{5,7},{6,4},{7,5},{8,72},{9,73},{10,... | collective-permute-start | bytes 294920 | tf_op jit(solution)/shard_map/ppermute | solution.py:32
  20.3 3.5 %collective-permute-start.3 = (bf16[2,96,256]{2,1,0:T(8,128)(2,1)S(1)}, bf16[2,96,256]{2,1,0:T(8,128)(2,1)S(1)}, u32[]{:S(2)}, u32[]{:S(2)}) collective-permute-start(bf16[2,96,256]{2,1,0:T(8,128)(2,1)S(1)} %get-tuple-element.8), channel_id=1, source_target_pairs={{0,3},{1,0},{2,1},{3,2},{4,7},{5,4},{6,5},{7,6},{8,104},{9,105},{1... | collective-permute-start | bytes 294920 | tf_op jit(solution)/shard_map/ppermute | solution.py:32
  23.8 4.3 %collective-permute-start.6 = (bf16[4,2,96,256]{3,2,1,0:T(8,128)(2,1)S(1)}, bf16[4,2,96,256]{3,2,1,0:T(8,128)(2,1)S(1)}, u32[]{:S(2)}, u32[]{:S(2)}) collective-permute-start(bf16[4,2,96,256]{3,2,1,0:T(8,128)(2,1)S(1)} %pad_maximum_fusion.1), channel_id=1, source_target_pairs={{0,8},{1,9},{2,10},{3,11},{4,12},{5,13},{6,14},{7,15},{8,0},{9,1},... | collective-permute-start | bytes 1179656 | tf_op jit(solution)/shard_map/ppermute | solution.py:32

commit v3 on v2

v3 whole, which is shorter than its diff:
```python
import jax
import jax.numpy as jnp
from jax import lax
from jax.experimental import pallas as pl
from jax.experimental.pallas import tpu as pltpu
from jax.sharding import PartitionSpec as P

EPS = 1e-06
LENGTH = 200
LAG = 64
REACH = 768
SPAN = 896
TAPS = 640
WIDE = 1024
ROWS = 8
SENDER = 1
PARTS = LENGTH // LAG + 1
GROUP = 128 // LAG
COLUMNS = 128 if 3 * LAG <= 128 else 256


def coordinates(time_index, station_index):
    return time_index // 4, (time_index // 2) % 2, time_index % 2, station_index // 4, station_index % 4


def exchange(value, templates_to, records_to):
    pairs = []
    for i in range(16):
        for j in range(8):
            target = (templates_to if i % 2 == SENDER else records_to)(*coordinates(i, j))
            x, y, core, high, z = target
            pairs.append((i * 8 + j, ((x * 2 + y) * 2 + core) * 8 + high * 4 + z))
    return lax.ppermute(value, ("tm", "sta"), pairs)


def other_core(x, y, core, high, z):
    return x, y, 1 - core, high, z


def to_owner(x, y, core, high, z):
    near, level = x // 2, x % 2 * 2 + y
    return (x + 2 + z - level) % 4, y ^ high ^ near, core, near, level


def to_previous(x, y, core, high, z):
    return (x - 1 + y) % 4, 1 - y, core, high, z


def to_owner_across(x, y, core, high, z):
    x, y, core, high, z = to_owner(x, y, core, high, z)
    return x, 1 - y, core, high, z


def to_previous_across(x, y, core, high, z):
    x, y, core, high, z = to_previous(x, y, core, high, z)
    return x, y, core, 1 - high, z


def across_y(x, y, core, high, z):
    return x, 1 - y, core, high, z


def across_high(x, y, core, high, z):
    return x, y, core, 1 - high, z


def back_x(steps):
    return lambda x, y, core, high, z: ((x - steps) % 4, y, core, high, z)


def back_z(steps):
    return lambda x, y, core, high, z: (x, y, core, high, (z - steps) % 4)


def take(value, index):
    return jnp.take_along_axis(value, index, axis=1)


def windows(series):
    return pltpu.roll(series, WIDE - LAG + 1, 1, stride=1, stride_axis=0)[:, :SPAN].astype(jnp.bfloat16)


def ahead(value, steps):
    return pltpu.roll(value, value.shape[1] - steps, 1)


def arrangement():
    source = lax.broadcasted_iota(jnp.int32, (TAPS, PARTS * COLUMNS), 0)
    column = lax.broadcasted_iota(jnp.int32, (TAPS, PARTS * COLUMNS), 1)
    place = column % COLUMNS
    lag = column // COLUMNS * LAG + LAG - 1 - place % LAG
    wanted = place // LAG * LENGTH + lag
    return jnp.where((source == wanted) & (lag < LENGTH) & (place < 3 * LAG), 1.0, 0.0).astype(jnp.bfloat16)


def kernel(gathered_ref, arrangement_ref, out_ref, scale_ref, lagged_ref, left_ref, moves_ref, chosen_ref, values_ref):
    i, j = lax.axis_index("tm"), lax.axis_index("sta")
    x, y, core, _, z = coordinates(i, j)
    sender = jnp.where(core == SENDER, 0, 1)
    template = lax.broadcasted_iota(jnp.int32, (16, 128), 0)
    lane = lax.broadcasted_iota(jnp.int32, (16, 128), 1)
    own = lane == template + 16 * j
    energies = []
    for slot in range(8):
        held = gathered_ref[1 - sender, slot // 2, slot % 2].astype(jnp.float32)
        pieces = [held[at : at + ROWS, :512] for at in (0, 8, 16)]
        wide = jnp.concatenate([jnp.where(core == 0, a, b) for a, b in zip(pieces[:-1], pieces[1:])], axis=1)
        squares = wide * wide
        energies.append(squares[0:2] + squares[2:4] + squares[4:6])
        for station in range(2):
            at = slot * 2 + station
            shifts = jnp.broadcast_to(held[24 + station : 25 + station, :128], (16, 128))
            chosen_ref[at * 16 : (at + 1) * 16] = jnp.where(own, shifts, 0.0).astype(jnp.bfloat16)
            for c in range(3):
                row = jnp.broadcast_to(wide[c * 2 + station : c * 2 + station + 1], (LAG, WIDE))
                lagged_ref[at, c * LAG : (c + 1) * LAG] = windows(row)
    energy = jnp.concatenate(energies, axis=0)
    four = energy + ahead(energy, 1) + (ahead(energy, 2) + ahead(energy, 3))
    eight = four + ahead(four, 4)
    sixteen = eight + (ahead(four, 8) + ahead(four, 12))
    sixty = sixteen + ahead(sixteen, 16) + (ahead(sixteen, 32) + ahead(sixteen, 48))
    total = sixty + ahead(sixty, 64) + (ahead(sixty, 128) + ahead(eight, 192))
    scale = lax.rsqrt(total[:, :REACH] + EPS)
    for row in range(16):
        scale_ref[row] = jnp.broadcast_to(scale[row : row + 1], (ROWS, REACH))

    moves_ref[...] = jnp.dot(
        chosen_ref[...], jnp.ones((128, 128), jnp.bfloat16), preferred_element_type=jnp.float32
    ).astype(jnp.int32)
    blocks = gathered_ref[sender].reshape(256, TAPS)
    left_ref[...] = jnp.dot(blocks, arrangement_ref[...], preferred_element_type=jnp.float32).astype(jnp.bfloat16)

    result = jnp.zeros((16, 512), jnp.float32)
    for dx in range(4):
        for dy in range(2):
            slot = lax.rem(x + dx - j // 2 + 6, 4) * 2 + lax.rem(y + dy + j, 2)
            for station in range(2):
                top = (dx * 2 + dy) * 32 + station * 16
                left = jnp.concatenate(
                    [left_ref[top : top + 16, a * COLUMNS : a * COLUMNS + 3 * LAG] for a in range(PARTS)], axis=0
                )
                at = slot * 2 + station
                sums = jnp.dot(left, lagged_ref[at], preferred_element_type=jnp.float32)
                parts = [sums[a * 16 : (a + 1) * 16] for a in range(PARTS)]
                values = None
                for group in range(GROUP - 1, -1, -1):
                    term = parts[group]
                    if group + GROUP < PARTS:
                        term = term[:, :REACH] + parts[group + GROUP][:, 128:]
                    values = term if values is None else term + ahead(values, LAG)[:, :REACH]
                values = values * jnp.concatenate([scale_ref[at]] * 2, axis=0)
                values_ref[(dx * 2 + dy) * 2 + station] = values
    for dx in range(4):
        for dy in range(2):
            slot = lax.rem(x + dx - j // 2 + 6, 4) * 2 + lax.rem(y + dy + j, 2)
            for station in range(2):
                values = values_ref[(dx * 2 + dy) * 2 + station]
                at = slot * 2 + station
                moves = moves_ref[pl.ds(pl.multiple_of(at * 16, 16), 16)]
                near = moves & 127
                picked = [values[:, at : at + 128] for at in range(0, REACH, 128)]
                picked = [jnp.where(moves >= 128, b, a) for a, b in zip(picked[:-1], picked[1:])]
                picked = [jnp.where(lane < near, b, a) for a, b in zip(picked[:-1], picked[1:])]
                index = (lane + near) & 127
                result += jnp.concatenate([take(value, index) for value in picked], axis=1)
    out_ref[...] = result


def bring(*refs):
    half = len(refs) // 2
    for source, target in zip(refs[:half], refs[half:]):
        target[...] = source[...]


def brought(*values):
    return pl.pallas_call(
        bring,
        out_shape=[pltpu.VMEM(value.shape, value.dtype) for value in values],
        in_specs=[pl.BlockSpec(memory_space=pltpu.VMEM)] * len(values),
        out_specs=[pl.BlockSpec(memory_space=pltpu.VMEM)] * len(values),
    )(*values)


def local(records, templates, moveouts):
    i = lax.axis_index("tm")
    first = i % 2 == SENDER
    records, templates, moveouts = brought(
        jnp.transpose(records, (1, 0, 2)), jnp.transpose(templates, (0, 2, 1, 3)), jnp.transpose(moveouts)
    )
    packet = jnp.pad(jnp.transpose(templates, (2, 0, 1, 3)).reshape(16, 3 * LENGTH), ((0, 0), (0, TAPS - 3 * LENGTH)))
    series = jnp.pad(records.reshape(6, 512), ((0, 2), (0, TAPS - 512)))
    shifts = jnp.pad(moveouts.astype(jnp.bfloat16), ((0, 6), (0, TAPS - 128)))
    series = jnp.concatenate([series, shifts], axis=0)
    came = exchange(jnp.where(first, series, packet), other_core, other_core)
    mine = jnp.where(first, packet, series)
    held = jnp.concatenate([came[:8], mine[:8], came[8:], mine[8:]], axis=0)
    one = exchange(held, to_owner, to_previous)
    two = exchange(held, to_owner_across, across_high)
    three = exchange(held, across_y, to_previous_across)
    order = arrangement()
    ends = i // 2 == 7
    near_after = jnp.where(ends, jnp.zeros_like(one[8:16]), one[8:16])
    far_after = jnp.where(ends, jnp.zeros_like(three[8:16]), three[8:16])
    near = jnp.where(first, one, jnp.concatenate([mine[:8], came[:8], near_after, mine[8:]], axis=0))
    far = jnp.where(first, two, jnp.concatenate([two[8:16], two[:8], far_after, two[24:]], axis=0))
    held = jnp.stack([near, far])
    held = jnp.stack([held] + [exchange(held, back_x(steps), back_z(steps)) for steps in (1, 2, 3)])
    held = jnp.stack([held, exchange(held, other_core, other_core)])

    return pl.pallas_call(
        kernel,
        out_shape=jax.ShapeDtypeStruct((16, 512), jnp.float32),
        in_specs=[pl.BlockSpec(memory_space=pltpu.VMEM)] * 2,
        out_specs=pl.BlockSpec(memory_space=pltpu.VMEM),
        scratch_shapes=[
            pltpu.VMEM((16, ROWS, REACH), jnp.float32),
            pltpu.VMEM((16, 3 * LAG, SPAN), jnp.bfloat16),
            pltpu.VMEM((256, PARTS * COLUMNS), jnp.bfloat16),
            pltpu.VMEM((256, 128), jnp.int32),
            pltpu.VMEM((256, 128), jnp.bfloat16),
            pltpu.VMEM((16, 16, REACH), jnp.float32),
        ],
        compiler_params=pltpu.CompilerParams(vmem_limit_bytes=40 * 1024 * 1024),
        cost_estimate=pl.CostEstimate(flops=2 * 128 * 2 * 600 * 696, bytes_accessed=600_000, transcendentals=0),
    )(held, order)


def solution(mesh):
    return jax.shard_map(
        local,
        mesh=mesh,
        in_specs=(P("sta", None, "tm"), P("tm", "sta", None, None), P(None, "sta")),
        out_specs=P("sta", "tm"),
        check_vma=False,
    )
```

time: 33.3 us -> 30.3 us (0.910); the launches traced: 32.8 us -> 30.2 us
  waiting for transfers between devices: 9.66 us -> 6.64 us
  local copies, waits for them, and re-layouts: 1.68 us -> 0.13 us
  starting transfers between devices: 16.2 us -> 17.7 us
    ppermute x7 -> x8, waiting for transfers between devices: 9.66 us -> 6.64 us  [exchange(): return lax.ppermute(value, ('tm', 'sta'), pairs)]
    ppermute x7 -> x8, starting transfers between devices: 16.2 us -> 17.7 us  [exchange(): return lax.ppermute(value, ('tm', 'sta'), pairs)]
    unnamed x9 -> x0, local copies, waits for them, and re-layouts: 1.42 us -> none
    pallas_call x0 -> x1, Pallas kernels: none -> 0.75 us  [brought(): pl.pallas_call(bring, out_shape=[pltpu.VMEM(value.shape, value.dtype) for...]
    pallas_call x1, Pallas kernels: 4.66 us -> 4.08 us  [local(): pl.pallas_call(kernel, out_shape=jax.ShapeDtypeStruct((16, 512), jnp.floa...]
    convert_element_type x0 -> x2, other arithmetic: none -> 0.52 us  [the longest x1 0.51 us: arrangement(): jnp.where((source == wanted) & (lag < LENGTH) & (place < 3 * LAG), 1.0, 0.0)]
  transfers between devices with their start and end apart: 7 -> 8, of which waited for: 7 -> 5; matrix products, arithmetic and copies ran while one was open for 0% -> 2% of each run, Pallas kernels for 0% -> 0%
where the time goes in v3:
time: 30.3 us; the launch traced here: 30.2 us
  starting transfers between devices  17.7 us (58%)
  waiting for transfers between devices  6.64 us (22%)
  Pallas kernels  4.83 us (16%)
  other arithmetic  0.76 us (3%)
    ppermute x8, starting transfers between devices, exchange(): return lax.ppermute(value, ('tm', 'sta'), pairs)  17.7 us
    ppermute x8, waiting for transfers between devices, exchange(): return lax.ppermute(value, ('tm', 'sta'), pairs)  6.64 us
    pallas_call x1, Pallas kernels, local(): pl.pallas_call(kernel, out_shape=jax.ShapeDtypeStruct((16, 512), jnp.floa...  4.08 us
    pallas_call x1, Pallas kernels, brought(): pl.pallas_call(bring, out_shape=[pltpu.VMEM(value.shape, value.dtype) for...  0.75 us
  transfers between devices with their start and end apart: 8, of which 5 were waited for; matrix products, arithmetic and copies ran while one was open for 2% of the time, Pallas kernels for 0%

profile of v3, /device:TPU:1, one launch (start us, length us, event | category | flops | bytes accessed | tf_op | source)
XLA Modules:
  0.0 30.2 jit_solution(9392928622678970552)
XLA Ops:
  0.0 0.7 %shard_map.37 = (bf16[3,2,512]{2,1,0:T(2,128)(2,1)S(1)}, bf16[8,3,2,200]{3,2,1,0:T(2,128)(2,1)S(1)}, s32[2,128]{1,0:T(2,128)S(1)}) custom-call(bf16[3,2,512]{2,1,0:T(2,128)(2,1)} %bitcast.22, bf16[8,3,2,200]{3,2,1,0:T(2,128)(2,1)} %bitcast.21, s32[2,128]{1,0:T(2,128)} %bitcast.23), custom_call_target="tpu_custom_call" | custom-call | tf_op jit(solution)/shard_map/pallas_call | solution.py:176
  0.8 0.1 reshape.7
  0.9 1.5 %collective-permute-start = (bf16[16,640]{1,0:T(8,128)(2,1)S(1)}, bf16[16,640]{1,0:T(8,128)(2,1)S(1)}, u32[]{:S(2)}, u32[]{:S(2)}) collective-permute-start(bf16[16,640]{1,0:T(8,128)(2,1)S(1)} %get-tuple-element.18), channel_id=1, source_target_pairs={{0,8},{1,9},{2,10},{3,11},{4,12},{5,13},{6,14},{7,15},{8,0},{9,1},... | collective-permute-start | bytes 61448 | tf_op jit(solution)/shard_map/ppermute | solution.py:33
  2.4 0.8 %collective-permute-done = bf16[16,640]{1,0:T(8,128)(2,1)S(1)} collective-permute-done((bf16[16,640]{1,0:T(8,128)(2,1)S(1)}, bf16[16,640]{1,0:T(8,128)(2,1)S(1)}, u32[]{:S(2)}, u32[]{:S(2)}) %collective-permute-start) | collective-permute-done | bytes 20512 | tf_op jit(solution)/shard_map/ppermute | solution.py:33
  3.3 3.9 %collective-permute-start.2 = (bf16[32,640]{1,0:T(8,128)(2,1)S(1)}, bf16[32,640]{1,0:T(8,128)(2,1)S(1)}, u32[]{:S(2)}, u32[]{:S(2)}) collective-permute-start(bf16[32,640]{1,0:T(8,128)(2,1)S(1)} %pad_maximum_fusion.4), channel_id=1, source_target_pairs={{0,4},{1,5},{2,6},{3,7},{4,0},{5,1},{6,2},{7,3},{8,88},{9,120},{10... | collective-permute-start | bytes 122888 | tf_op jit(solution)/shard_map/ppermute | solution.py:33
  7.2 0.0 collective-permute-start.3
  7.2 4.3 %collective-permute-start.1 = (bf16[32,640]{1,0:T(8,128)(2,1)S(1)}, bf16[32,640]{1,0:T(8,128)(2,1)S(1)}, u32[]{:S(2)}, u32[]{:S(2)}) collective-permute-start(bf16[32,640]{1,0:T(8,128)(2,1)S(1)} %pad_maximum_fusion.4), channel_id=1, source_target_pairs={{0,112},{1,113},{2,114},{3,115},{4,116},{5,117},{6,118},{7,119},{8... | collective-permute-start | bytes 122888 | tf_op jit(solution)/shard_map/ppermute | solution.py:33
  11.5 0.0 collective-permute-done.2
  11.5 0.0 collective-permute-done.3
  11.5 1.1 %collective-permute-done.1 = bf16[32,640]{1,0:T(8,128)(2,1)S(1)} collective-permute-done((bf16[32,640]{1,0:T(8,128)(2,1)S(1)}, bf16[32,640]{1,0:T(8,128)(2,1)S(1)}, u32[]{:S(2)}, u32[]{:S(2)}) %collective-permute-start.1) | collective-permute-done | bytes 40992 | tf_op jit(solution)/shard_map/ppermute | solution.py:33
  12.6 3.3 %collective-permute-start.5 = (bf16[2,32,640]{2,1,0:T(8,128)(2,1)S(1)}, bf16[2,32,640]{2,1,0:T(8,128)(2,1)S(1)}, u32[]{:S(2)}, u32[]{:S(2)}) collective-permute-start(bf16[2,32,640]{2,1,0:T(8,128)(2,1)S(1)} %get-tuple-element.14), channel_id=1, source_target_pairs={{0,2},{1,3},{2,0},{3,1},{4,6},{5,7},{6,4},{7,5},{8,72},{9,73},{10,... | collective-permute-start | bytes 245768 | tf_op jit(solution)/shard_map/ppermute | solution.py:33
  16.0 2.2 %collective-permute-start.4 = (bf16[2,32,640]{2,1,0:T(8,128)(2,1)S(1)}, bf16[2,32,640]{2,1,0:T(8,128)(2,1)S(1)}, u32[]{:S(2)}, u32[]{:S(2)}) collective-permute-start(bf16[2,32,640]{2,1,0:T(8,128)(2,1)S(1)} %get-tuple-element.14), channel_id=1, source_target_pairs={{0,3},{1,0},{2,1},{3,2},{4,7},{5,4},{6,5},{7,6},{8,104},{9,105},{1... | collective-permute-start | bytes 245768 | tf_op jit(solution)/shard_map/ppermute | solution.py:33
  18.1 0.5 %collective-permute-start.6 = (bf16[2,32,640]{2,1,0:T(8,128)(2,1)S(1)}, bf16[2,32,640]{2,1,0:T(8,128)(2,1)S(1)}, u32[]{:S(2)}, u32[]{:S(2)}) collective-permute-start(bf16[2,32,640]{2,1,0:T(8,128)(2,1)S(1)} %get-tuple-element.14), channel_id=1, source_target_pairs={{0,1},{1,2},{2,3},{3,0},{4,5},{5,6},{6,7},{7,4},{8,40},{9,41},{10,... | collective-permute-start | bytes 245768 | tf_op jit(solution)/shard_map/ppermute | solution.py:33
  18.7 0.0 collective-permute-done.5
  18.7 3.0 %collective-permute-done.4 = bf16[2,32,640]{2,1,0:T(8,128)(2,1)S(1)} collective-permute-done((bf16[2,32,640]{2,1,0:T(8,128)(2,1)S(1)}, bf16[2,32,640]{2,1,0:T(8,128)(2,1)S(1)}, u32[]{:S(2)}, u32[]{:S(2)}) %collective-permute-start.4) | collective-permute-done | bytes 81952 | tf_op jit(solution)/shard_map/ppermute | solution.py:33
  21.6 1.0 %collective-permute-done.6 = bf16[2,32,640]{2,1,0:T(8,128)(2,1)S(1)} collective-permute-done((bf16[2,32,640]{2,1,0:T(8,128)(2,1)S(1)}, bf16[2,32,640]{2,1,0:T(8,128)(2,1)S(1)}, u32[]{:S(2)}, u32[]{:S(2)}) %collective-permute-start.6) | collective-permute-done | bytes 81952 | tf_op jit(solution)/shard_map/ppermute | solution.py:33
  22.7 0.1 fusion.22
  22.7 2.0 %collective-permute-start.7 = (bf16[4,2,32,640]{3,2,1,0:T(8,128)(2,1)S(1)}, bf16[4,2,32,640]{3,2,1,0:T(8,128)(2,1)S(1)}, u32[]{:S(2)}, u32[]{:S(2)}) collective-permute-start(bf16[4,2,32,640]{3,2,1,0:T(8,128)(2,1)S(1)} %get-tuple-element.12), channel_id=1, source_target_pairs={{0,8},{1,9},{2,10},{3,11},{4,12},{5,13},{6,14},{7,15},{8,0},{9,1},... | collective-permute-start | bytes 983048 | tf_op jit(solution)/shard_map/ppermute | solution.py:33
  24.8 0.5 %select_convert_fusion.arrangement_ref = bf16[640,1024]{1,0:T(8,128)(2,1)S(1)} fusion(s32[1024]{0:T(1024)S(1)} %get-tuple-element.24, s32[1024]{0:T(1024)S(1)} %get-tuple-element.27, s32[1024]{0:T(1024)S(1)} %get-tuple-element.25, s32[1024]{0:T(1024)S(1)} %get-tuple-element.26, pred[1024]{0:T(1024)(128)(4,1)S(1)} %get-tuple-element.28, ...), kind=kLoop, calls=%fused_computation.16 | loop fusion | flops 21626880 | bytes 1329152 | tf_op jit(solution)/shard_map/convert_element_type | solution.py:93
  25.3 0.7 %collective-permute-done.7 = bf16[4,2,32,640]{3,2,1,0:T(8,128)(2,1)S(1)} collective-permute-done((bf16[4,2,32,640]{3,2,1,0:T(8,128)(2,1)S(1)}, bf16[4,2,32,640]{3,2,1,0:T(8,128)(2,1)S(1)}, u32[]{:S(2)}, u32[]{:S(2)}) %collective-permute-start.7) | collective-permute-done | bytes 327712 | tf_op jit(solution)/shard_map/ppermute | solution.py:33
  26.0 0.1 pad_maximum_fusion.gathered_ref
  26.1 4.1 %shard_map.38 = f32[16,512]{1,0:T(8,128)} custom-call(bf16[2,4,2,32,640]{4,3,2,1,0:T(8,128)(2,1)S(1)} %pad_maximum_fusion.gathered_ref, bf16[640,1024]{1,0:T(8,128)(2,1)S(1)} %select_convert_fusion.arrangement_ref), custom_call_target="tpu_custom_call" | custom-call | flops 213811200 | bytes 600000 | tf_op jit(solution)/shard_map/pallas_call | solution.py:210
  (16 shorter events, 0.1 us)
Async XLA Ops:
  0.9 2.3 %collective-permute-start = (bf16[16,640]{1,0:T(8,128)(2,1)S(1)}, bf16[16,640]{1,0:T(8,128)(2,1)S(1)}, u32[]{:S(2)}, u32[]{:S(2)}) collective-permute-start(bf16[16,640]{1,0:T(8,128)(2,1)S(1)} %get-tuple-element.18), channel_id=1, source_target_pairs={{0,8},{1,9},{2,10},{3,11},{4,12},{5,13},{6,14},{7,15},{8,0},{9,1},... | collective-permute-start | bytes 61448 | tf_op jit(solution)/shard_map/ppermute | solution.py:33
  3.3 8.2 %collective-permute-start.2 = (bf16[32,640]{1,0:T(8,128)(2,1)S(1)}, bf16[32,640]{1,0:T(8,128)(2,1)S(1)}, u32[]{:S(2)}, u32[]{:S(2)}) collective-permute-start(bf16[32,640]{1,0:T(8,128)(2,1)S(1)} %pad_maximum_fusion.4), channel_id=1, source_target_pairs={{0,4},{1,5},{2,6},{3,7},{4,0},{5,1},{6,2},{7,3},{8,88},{9,120},{10... | collective-permute-start | bytes 122888 | tf_op jit(solution)/shard_map/ppermute | solution.py:33
  7.2 4.3 %collective-permute-start.3 = (bf16[32,640]{1,0:T(8,128)(2,1)S(1)}, bf16[32,640]{1,0:T(8,128)(2,1)S(1)}, u32[]{:S(2)}, u32[]{:S(2)}) collective-permute-start(bf16[32,640]{1,0:T(8,128)(2,1)S(1)} %pad_maximum_fusion.4), channel_id=1, source_target_pairs={{0,116},{1,117},{2,118},{3,119},{4,112},{5,113},{6,114},{7,115},{8... | collective-permute-start | bytes 122888 | tf_op jit(solution)/shard_map/ppermute | solution.py:33
  7.2 5.4 %collective-permute-start.1 = (bf16[32,640]{1,0:T(8,128)(2,1)S(1)}, bf16[32,640]{1,0:T(8,128)(2,1)S(1)}, u32[]{:S(2)}, u32[]{:S(2)}) collective-permute-start(bf16[32,640]{1,0:T(8,128)(2,1)S(1)} %pad_maximum_fusion.4), channel_id=1, source_target_pairs={{0,112},{1,113},{2,114},{3,115},{4,116},{5,117},{6,118},{7,119},{8... | collective-permute-start | bytes 122888 | tf_op jit(solution)/shard_map/ppermute | solution.py:33
  12.6 6.0 %collective-permute-start.5 = (bf16[2,32,640]{2,1,0:T(8,128)(2,1)S(1)}, bf16[2,32,640]{2,1,0:T(8,128)(2,1)S(1)}, u32[]{:S(2)}, u32[]{:S(2)}) collective-permute-start(bf16[2,32,640]{2,1,0:T(8,128)(2,1)S(1)} %get-tuple-element.14), channel_id=1, source_target_pairs={{0,2},{1,3},{2,0},{3,1},{4,6},{5,7},{6,4},{7,5},{8,72},{9,73},{10,... | collective-permute-start | bytes 245768 | tf_op jit(solution)/shard_map/ppermute | solution.py:33
  16.0 5.7 %collective-permute-start.4 = (bf16[2,32,640]{2,1,0:T(8,128)(2,1)S(1)}, bf16[2,32,640]{2,1,0:T(8,128)(2,1)S(1)}, u32[]{:S(2)}, u32[]{:S(2)}) collective-permute-start(bf16[2,32,640]{2,1,0:T(8,128)(2,1)S(1)} %get-tuple-element.14), channel_id=1, source_target_pairs={{0,3},{1,0},{2,1},{3,2},{4,7},{5,4},{6,5},{7,6},{8,104},{9,105},{1... | collective-permute-start | bytes 245768 | tf_op jit(solution)/shard_map/ppermute | solution.py:33
  18.1 4.5 %collective-permute-start.6 = (bf16[2,32,640]{2,1,0:T(8,128)(2,1)S(1)}, bf16[2,32,640]{2,1,0:T(8,128)(2,1)S(1)}, u32[]{:S(2)}, u32[]{:S(2)}) collective-permute-start(bf16[2,32,640]{2,1,0:T(8,128)(2,1)S(1)} %get-tuple-element.14), channel_id=1, source_target_pairs={{0,1},{1,2},{2,3},{3,0},{4,5},{5,6},{6,7},{7,4},{8,40},{9,41},{10,... | collective-permute-start | bytes 245768 | tf_op jit(solution)/shard_map/ppermute | solution.py:33
  22.7 3.3 %collective-permute-start.7 = (bf16[4,2,32,640]{3,2,1,0:T(8,128)(2,1)S(1)}, bf16[4,2,32,640]{3,2,1,0:T(8,128)(2,1)S(1)}, u32[]{:S(2)}, u32[]{:S(2)}) collective-permute-start(bf16[4,2,32,640]{3,2,1,0:T(8,128)(2,1)S(1)} %get-tuple-element.12), channel_id=1, source_target_pairs={{0,8},{1,9},{2,10},{3,11},{4,12},{5,13},{6,14},{7,15},{8,0},{9,1},... | collective-permute-start | bytes 983048 | tf_op jit(solution)/shard_map/ppermute | solution.py:33

commit v4 on v3

--- a/solution.py
+++ b/solution.py
@@ -102,7 +102,9 @@
     own = lane == template + 16 * j
     energies = []
     for slot in range(8):
-        held = gathered_ref[1 - sender, slot // 2, slot % 2].astype(jnp.float32)
+        level = lax.rem(x + slot // 2 - j // 2 + 6, 4)
+        half = lax.rem(y + slot % 2 + j, 2)
+        held = gathered_ref[1 - sender, level, half].astype(jnp.float32)
         pieces = [held[at : at + ROWS, :512] for at in (0, 8, 16)]
         wide = jnp.concatenate([jnp.where(core == 0, a, b) for a, b in zip(pieces[:-1], pieces[1:])], axis=1)
         squares = wide * wide
@@ -133,13 +135,12 @@
     result = jnp.zeros((16, 512), jnp.float32)
     for dx in range(4):
         for dy in range(2):
-            slot = lax.rem(x + dx - j // 2 + 6, 4) * 2 + lax.rem(y + dy + j, 2)
             for station in range(2):
-                top = (dx * 2 + dy) * 32 + station * 16
+                at = (dx * 2 + dy) * 2 + station
+                top = at * 16
                 left = jnp.concatenate(
                     [left_ref[top : top + 16, a * COLUMNS : a * COLUMNS + 3 * LAG] for a in range(PARTS)], axis=0
                 )
-                at = slot * 2 + station
                 sums = jnp.dot(left, lagged_ref[at], preferred_element_type=jnp.float32)
                 parts = [sums[a * 16 : (a + 1) * 16] for a in range(PARTS)]
                 values = None
@@ -149,20 +150,16 @@
                         term = term[:, :REACH] + parts[group + GROUP][:, 128:]
                     values = term if values is None else term + ahead(values, LAG)[:, :REACH]
                 values = values * jnp.concatenate([scale_ref[at]] * 2, axis=0)
-                values_ref[(dx * 2 + dy) * 2 + station] = values
-    for dx in range(4):
-        for dy in range(2):
-            slot = lax.rem(x + dx - j // 2 + 6, 4) * 2 + lax.rem(y + dy + j, 2)
-            for station in range(2):
-                values = values_ref[(dx * 2 + dy) * 2 + station]
-                at = slot * 2 + station
-                moves = moves_ref[pl.ds(pl.multiple_of(at * 16, 16), 16)]
-                near = moves & 127
-                picked = [values[:, at : at + 128] for at in range(0, REACH, 128)]
-                picked = [jnp.where(moves >= 128, b, a) for a, b in zip(picked[:-1], picked[1:])]
-                picked = [jnp.where(lane < near, b, a) for a, b in zip(picked[:-1], picked[1:])]
-                index = (lane + near) & 127
-                result += jnp.concatenate([take(value, index) for value in picked], axis=1)
+                values_ref[at] = values
+    for at in range(16):
+        values = values_ref[at]
+        moves = moves_ref[at * 16 : (at + 1) * 16]
+        near = moves & 127
+        picked = [values[:, q : q + 128] for q in range(0, REACH, 128)]
+        picked = [jnp.where(moves >= 128, b, a) for a, b in zip(picked[:-1], picked[1:])]
+        picked = [jnp.where(lane < near, b, a) for a, b in zip(picked[:-1], picked[1:])]
+        index = (lane + near) & 127
+        result += jnp.concatenate([take(value, index) for value in picked], axis=1)
     out_ref[...] = result
 
 
@@ -191,16 +188,16 @@
     series = jnp.pad(records.reshape(6, 512), ((0, 2), (0, TAPS - 512)))
     shifts = jnp.pad(moveouts.astype(jnp.bfloat16), ((0, 6), (0, TAPS - 128)))
     series = jnp.concatenate([series, shifts], axis=0)
+    mine = jnp.where(first, packet, series)
     came = exchange(jnp.where(first, series, packet), other_core, other_core)
-    mine = jnp.where(first, packet, series)
+    three = exchange(mine, across_y, to_previous_across)
     held = jnp.concatenate([came[:8], mine[:8], came[8:], mine[8:]], axis=0)
     one = exchange(held, to_owner, to_previous)
     two = exchange(held, to_owner_across, across_high)
-    three = exchange(held, across_y, to_previous_across)
     order = arrangement()
     ends = i // 2 == 7
     near_after = jnp.where(ends, jnp.zeros_like(one[8:16]), one[8:16])
-    far_after = jnp.where(ends, jnp.zeros_like(three[8:16]), three[8:16])
+    far_after = jnp.where(ends, jnp.zeros_like(three[:8]), three[:8])
     near = jnp.where(first, one, jnp.concatenate([mine[:8], came[:8], near_after, mine[8:]], axis=0))
     far = jnp.where(first, two, jnp.concatenate([two[8:16], two[:8], far_after, two[24:]], axis=0))
     held = jnp.stack([near, far])

time: 30.3 us -> 29.4 us (0.970)
  starting transfers between devices: 17.7 us -> 16.6 us
  waiting for transfers between devices: 6.64 us -> 7.26 us
  Pallas kernels: 4.83 us -> 4.3 us
    ppermute x8, starting transfers between devices: 17.7 us -> 16.6 us  [exchange(): return lax.ppermute(value, ('tm', 'sta'), pairs)]
    ppermute x8, waiting for transfers between devices: 6.64 us -> 7.26 us  [exchange(): return lax.ppermute(value, ('tm', 'sta'), pairs)]
    pallas_call x1, Pallas kernels: 4.08 us -> 3.55 us  [local(): pl.pallas_call(kernel, out_shape=jax.ShapeDtypeStruct((16, 512), jnp.floa...]
where the time goes in v4:
time: 29.4 us; the launch traced here: 29.2 us
  starting transfers between devices  16.6 us (56%)
  waiting for transfers between devices  7.26 us (25%)
  Pallas kernels  4.3 us (15%)
  other arithmetic  0.75 us (3%)
    ppermute x8, starting transfers between devices, exchange(): return lax.ppermute(value, ('tm', 'sta'), pairs)  16.6 us
    ppermute x8, waiting for transfers between devices, exchange(): return lax.ppermute(value, ('tm', 'sta'), pairs)  7.26 us
    pallas_call x1, Pallas kernels, local(): pl.pallas_call(kernel, out_shape=jax.ShapeDtypeStruct((16, 512), jnp.floa...  3.55 us
    pallas_call x1, Pallas kernels, brought(): pl.pallas_call(bring, out_shape=[pltpu.VMEM(value.shape, value.dtype) for...  0.75 us
  transfers between devices with their start and end apart: 8, of which 5 were waited for; matrix products, arithmetic and copies ran while one was open for 2% of the time, Pallas kernels for 0%

profile of v4, /device:TPU:1, one launch (start us, length us, event | category | flops | bytes accessed | tf_op | source)
XLA Modules:
  0.0 29.2 jit_solution(11332031609118983111)
XLA Ops:
  0.0 0.7 %shard_map.37 = (bf16[3,2,512]{2,1,0:T(2,128)(2,1)S(1)}, bf16[8,3,2,200]{3,2,1,0:T(2,128)(2,1)S(1)}, s32[2,128]{1,0:T(2,128)S(1)}) custom-call(bf16[3,2,512]{2,1,0:T(2,128)(2,1)} %bitcast.22, bf16[8,3,2,200]{3,2,1,0:T(2,128)(2,1)} %bitcast.21, s32[2,128]{1,0:T(2,128)} %bitcast.23), custom_call_target="tpu_custom_call" | custom-call | tf_op jit(solution)/shard_map/pallas_call | solution.py:173
  0.8 0.1 reshape.7
  0.9 1.5 %collective-permute-start = (bf16[16,640]{1,0:T(8,128)(2,1)S(1)}, bf16[16,640]{1,0:T(8,128)(2,1)S(1)}, u32[]{:S(2)}, u32[]{:S(2)}) collective-permute-start(bf16[16,640]{1,0:T(8,128)(2,1)S(1)} %get-tuple-element.18), channel_id=1, source_target_pairs={{0,8},{1,9},{2,10},{3,11},{4,12},{5,13},{6,14},{7,15},{8,0},{9,1},... | collective-permute-start | bytes 61448 | tf_op jit(solution)/shard_map/ppermute | solution.py:33
  2.4 1.4 %collective-permute-start.3 = (bf16[16,640]{1,0:T(8,128)(2,1)S(1)}, bf16[16,640]{1,0:T(8,128)(2,1)S(1)}, u32[]{:S(2)}, u32[]{:S(2)}) collective-permute-start(bf16[16,640]{1,0:T(8,128)(2,1)S(1)} %get-tuple-element.19), channel_id=1, source_target_pairs={{0,116},{1,117},{2,118},{3,119},{4,112},{5,113},{6,114},{7,115},{8... | collective-permute-start | bytes 61448 | tf_op jit(solution)/shard_map/ppermute | solution.py:33
  3.8 0.0 collective-permute-done
  3.9 3.3 %collective-permute-start.2 = (bf16[32,640]{1,0:T(8,128)(2,1)S(1)}, bf16[32,640]{1,0:T(8,128)(2,1)S(1)}, u32[]{:S(2)}, u32[]{:S(2)}) collective-permute-start(bf16[32,640]{1,0:T(8,128)(2,1)S(1)} %pad_maximum_fusion.4), channel_id=1, source_target_pairs={{0,4},{1,5},{2,6},{3,7},{4,0},{5,1},{6,2},{7,3},{8,88},{9,120},{10... | collective-permute-start | bytes 122888 | tf_op jit(solution)/shard_map/ppermute | solution.py:33
  7.2 2.1 %collective-permute-start.1 = (bf16[32,640]{1,0:T(8,128)(2,1)S(1)}, bf16[32,640]{1,0:T(8,128)(2,1)S(1)}, u32[]{:S(2)}, u32[]{:S(2)}) collective-permute-start(bf16[32,640]{1,0:T(8,128)(2,1)S(1)} %pad_maximum_fusion.4), channel_id=1, source_target_pairs={{0,112},{1,113},{2,114},{3,115},{4,116},{5,117},{6,118},{7,119},{8... | collective-permute-start | bytes 122888 | tf_op jit(solution)/shard_map/ppermute | solution.py:33
  9.2 0.0 collective-permute-done.3
  9.2 2.1 %collective-permute-done.2 = bf16[32,640]{1,0:T(8,128)(2,1)S(1)} collective-permute-done((bf16[32,640]{1,0:T(8,128)(2,1)S(1)}, bf16[32,640]{1,0:T(8,128)(2,1)S(1)}, u32[]{:S(2)}, u32[]{:S(2)}) %collective-permute-start.2) | collective-permute-done | bytes 40992 | tf_op jit(solution)/shard_map/ppermute | solution.py:33
  11.4 0.4 %collective-permute-done.1 = bf16[32,640]{1,0:T(8,128)(2,1)S(1)} collective-permute-done((bf16[32,640]{1,0:T(8,128)(2,1)S(1)}, bf16[32,640]{1,0:T(8,128)(2,1)S(1)}, u32[]{:S(2)}, u32[]{:S(2)}) %collective-permute-start.1) | collective-permute-done | bytes 40992 | tf_op jit(solution)/shard_map/ppermute | solution.py:33
  11.9 2.2 %collective-permute-start.5 = (bf16[2,32,640]{2,1,0:T(8,128)(2,1)S(1)}, bf16[2,32,640]{2,1,0:T(8,128)(2,1)S(1)}, u32[]{:S(2)}, u32[]{:S(2)}) collective-permute-start(bf16[2,32,640]{2,1,0:T(8,128)(2,1)S(1)} %get-tuple-element.14), channel_id=1, source_target_pairs={{0,2},{1,3},{2,0},{3,1},{4,6},{5,7},{6,4},{7,5},{8,72},{9,73},{10,... | collective-permute-start | bytes 245768 | tf_op jit(solution)/shard_map/ppermute | solution.py:33
  14.0 3.5 %collective-permute-start.4 = (bf16[2,32,640]{2,1,0:T(8,128)(2,1)S(1)}, bf16[2,32,640]{2,1,0:T(8,128)(2,1)S(1)}, u32[]{:S(2)}, u32[]{:S(2)}) collective-permute-start(bf16[2,32,640]{2,1,0:T(8,128)(2,1)S(1)} %get-tuple-element.14), channel_id=1, source_target_pairs={{0,3},{1,0},{2,1},{3,2},{4,7},{5,4},{6,5},{7,6},{8,104},{9,105},{1... | collective-permute-start | bytes 245768 | tf_op jit(solution)/shard_map/ppermute | solution.py:33
  17.5 0.5 %collective-permute-start.6 = (bf16[2,32,640]{2,1,0:T(8,128)(2,1)S(1)}, bf16[2,32,640]{2,1,0:T(8,128)(2,1)S(1)}, u32[]{:S(2)}, u32[]{:S(2)}) collective-permute-start(bf16[2,32,640]{2,1,0:T(8,128)(2,1)S(1)} %get-tuple-element.14), channel_id=1, source_target_pairs={{0,1},{1,2},{2,3},{3,0},{4,5},{5,6},{6,7},{7,4},{8,40},{9,41},{10,... | collective-permute-start | bytes 245768 | tf_op jit(solution)/shard_map/ppermute | solution.py:33
  18.1 0.0 collective-permute-done.5
  18.1 3.0 %collective-permute-done.4 = bf16[2,32,640]{2,1,0:T(8,128)(2,1)S(1)} collective-permute-done((bf16[2,32,640]{2,1,0:T(8,128)(2,1)S(1)}, bf16[2,32,640]{2,1,0:T(8,128)(2,1)S(1)}, u32[]{:S(2)}, u32[]{:S(2)}) %collective-permute-start.4) | collective-permute-done | bytes 81952 | tf_op jit(solution)/shard_map/ppermute | solution.py:33
  21.0 1.0 %collective-permute-done.6 = bf16[2,32,640]{2,1,0:T(8,128)(2,1)S(1)} collective-permute-done((bf16[2,32,640]{2,1,0:T(8,128)(2,1)S(1)}, bf16[2,32,640]{2,1,0:T(8,128)(2,1)S(1)}, u32[]{:S(2)}, u32[]{:S(2)}) %collective-permute-start.6) | collective-permute-done | bytes 81952 | tf_op jit(solution)/shard_map/ppermute | solution.py:33
  22.0 0.1 fusion.22
  22.1 2.2 %collective-permute-start.7 = (bf16[4,2,32,640]{3,2,1,0:T(8,128)(2,1)S(1)}, bf16[4,2,32,640]{3,2,1,0:T(8,128)(2,1)S(1)}, u32[]{:S(2)}, u32[]{:S(2)}) collective-permute-start(bf16[4,2,32,640]{3,2,1,0:T(8,128)(2,1)S(1)} %get-tuple-element.12), channel_id=1, source_target_pairs={{0,8},{1,9},{2,10},{3,11},{4,12},{5,13},{6,14},{7,15},{8,0},{9,1},... | collective-permute-start | bytes 983048 | tf_op jit(solution)/shard_map/ppermute | solution.py:33
  24.3 0.5 %select_convert_fusion.arrangement_ref = bf16[640,1024]{1,0:T(8,128)(2,1)S(1)} fusion(s32[1024]{0:T(1024)S(1)} %get-tuple-element.24, s32[1024]{0:T(1024)S(1)} %get-tuple-element.27, s32[1024]{0:T(1024)S(1)} %get-tuple-element.25, s32[1024]{0:T(1024)S(1)} %get-tuple-element.26, pred[1024]{0:T(1024)(128)(4,1)S(1)} %get-tuple-element.28, ...), kind=kLoop, calls=%fused_computation.16 | loop fusion | flops 21626880 | bytes 1329152 | tf_op jit(solution)/shard_map/convert_element_type | solution.py:93
  24.8 0.7 %collective-permute-done.7 = bf16[4,2,32,640]{3,2,1,0:T(8,128)(2,1)S(1)} collective-permute-done((bf16[4,2,32,640]{3,2,1,0:T(8,128)(2,1)S(1)}, bf16[4,2,32,640]{3,2,1,0:T(8,128)(2,1)S(1)}, u32[]{:S(2)}, u32[]{:S(2)}) %collective-permute-start.7) | collective-permute-done | bytes 327712 | tf_op jit(solution)/shard_map/ppermute | solution.py:33
  25.6 0.1 pad_maximum_fusion.gathered_ref
  25.6 3.6 %shard_map.38 = f32[16,512]{1,0:T(8,128)} custom-call(bf16[2,4,2,32,640]{4,3,2,1,0:T(8,128)(2,1)S(1)} %pad_maximum_fusion.gathered_ref, bf16[640,1024]{1,0:T(8,128)(2,1)S(1)} %select_convert_fusion.arrangement_ref), custom_call_target="tpu_custom_call" | custom-call | flops 213811200 | bytes 600000 | tf_op jit(solution)/shard_map/pallas_call | solution.py:207
  (16 shorter events, 0.1 us)
Async XLA Ops:
  0.9 2.9 %collective-permute-start = (bf16[16,640]{1,0:T(8,128)(2,1)S(1)}, bf16[16,640]{1,0:T(8,128)(2,1)S(1)}, u32[]{:S(2)}, u32[]{:S(2)}) collective-permute-start(bf16[16,640]{1,0:T(8,128)(2,1)S(1)} %get-tuple-element.18), channel_id=1, source_target_pairs={{0,8},{1,9},{2,10},{3,11},{4,12},{5,13},{6,14},{7,15},{8,0},{9,1},... | collective-permute-start | bytes 61448 | tf_op jit(solution)/shard_map/ppermute | solution.py:33
  2.4 6.8 %collective-permute-start.3 = (bf16[16,640]{1,0:T(8,128)(2,1)S(1)}, bf16[16,640]{1,0:T(8,128)(2,1)S(1)}, u32[]{:S(2)}, u32[]{:S(2)}) collective-permute-start(bf16[16,640]{1,0:T(8,128)(2,1)S(1)} %get-tuple-element.19), channel_id=1, source_target_pairs={{0,116},{1,117},{2,118},{3,119},{4,112},{5,113},{6,114},{7,115},{8... | collective-permute-start | bytes 61448 | tf_op jit(solution)/shard_map/ppermute | solution.py:33
  3.9 7.5 %collective-permute-start.2 = (bf16[32,640]{1,0:T(8,128)(2,1)S(1)}, bf16[32,640]{1,0:T(8,128)(2,1)S(1)}, u32[]{:S(2)}, u32[]{:S(2)}) collective-permute-start(bf16[32,640]{1,0:T(8,128)(2,1)S(1)} %pad_maximum_fusion.4), channel_id=1, source_target_pairs={{0,4},{1,5},{2,6},{3,7},{4,0},{5,1},{6,2},{7,3},{8,88},{9,120},{10... | collective-permute-start | bytes 122888 | tf_op jit(solution)/shard_map/ppermute | solution.py:33
  7.2 4.6 %collective-permute-start.1 = (bf16[32,640]{1,0:T(8,128)(2,1)S(1)}, bf16[32,640]{1,0:T(8,128)(2,1)S(1)}, u32[]{:S(2)}, u32[]{:S(2)}) collective-permute-start(bf16[32,640]{1,0:T(8,128)(2,1)S(1)} %pad_maximum_fusion.4), channel_id=1, source_target_pairs={{0,112},{1,113},{2,114},{3,115},{4,116},{5,117},{6,118},{7,119},{8... | collective-permute-start | bytes 122888 | tf_op jit(solution)/shard_map/ppermute | solution.py:33
  11.9 6.2 %collective-permute-start.5 = (bf16[2,32,640]{2,1,0:T(8,128)(2,1)S(1)}, bf16[2,32,640]{2,1,0:T(8,128)(2,1)S(1)}, u32[]{:S(2)}, u32[]{:S(2)}) collective-permute-start(bf16[2,32,640]{2,1,0:T(8,128)(2,1)S(1)} %get-tuple-element.14), channel_id=1, source_target_pairs={{0,2},{1,3},{2,0},{3,1},{4,6},{5,7},{6,4},{7,5},{8,72},{9,73},{10,... | collective-permute-start | bytes 245768 | tf_op jit(solution)/shard_map/ppermute | solution.py:33
  14.0 7.0 %collective-permute-start.4 = (bf16[2,32,640]{2,1,0:T(8,128)(2,1)S(1)}, bf16[2,32,640]{2,1,0:T(8,128)(2,1)S(1)}, u32[]{:S(2)}, u32[]{:S(2)}) collective-permute-start(bf16[2,32,640]{2,1,0:T(8,128)(2,1)S(1)} %get-tuple-element.14), channel_id=1, source_target_pairs={{0,3},{1,0},{2,1},{3,2},{4,7},{5,4},{6,5},{7,6},{8,104},{9,105},{1... | collective-permute-start | bytes 245768 | tf_op jit(solution)/shard_map/ppermute | solution.py:33
  17.5 4.5 %collective-permute-start.6 = (bf16[2,32,640]{2,1,0:T(8,128)(2,1)S(1)}, bf16[2,32,640]{2,1,0:T(8,128)(2,1)S(1)}, u32[]{:S(2)}, u32[]{:S(2)}) collective-permute-start(bf16[2,32,640]{2,1,0:T(8,128)(2,1)S(1)} %get-tuple-element.14), channel_id=1, source_target_pairs={{0,1},{1,2},{2,3},{3,0},{4,5},{5,6},{6,7},{7,4},{8,40},{9,41},{10,... | collective-permute-start | bytes 245768 | tf_op jit(solution)/shard_map/ppermute | solution.py:33
  22.1 3.5 %collective-permute-start.7 = (bf16[4,2,32,640]{3,2,1,0:T(8,128)(2,1)S(1)}, bf16[4,2,32,640]{3,2,1,0:T(8,128)(2,1)S(1)}, u32[]{:S(2)}, u32[]{:S(2)}) collective-permute-start(bf16[4,2,32,640]{3,2,1,0:T(8,128)(2,1)S(1)} %get-tuple-element.12), channel_id=1, source_target_pairs={{0,8},{1,9},{2,10},{3,11},{4,12},{5,13},{6,14},{7,15},{8,0},{9,1},... | collective-permute-start | bytes 983048 | tf_op jit(solution)/shard_map/ppermute | solution.py:33

commit v5 on v4

--- a/solution.py
+++ b/solution.py
@@ -52,8 +52,15 @@
 
 
 def to_previous_across(x, y, core, high, z):
-    x, y, core, high, z = to_previous(x, y, core, high, z)
-    return x, y, core, 1 - high, z
+    if x + y == 0:
+        return x, y, 1 - core, high, z
+    return x - 1 + y, 1 - y, core, 1 - high, z
+
+
+def to_next(x, y, core, high, z):
+    if x * 2 + y == 7:
+        return x, y, 1 - core, high, z
+    return x + y, 1 - y, core, high, z
 
 
 def across_y(x, y, core, high, z):
@@ -190,7 +197,7 @@
     series = jnp.concatenate([series, shifts], axis=0)
     mine = jnp.where(first, packet, series)
     came = exchange(jnp.where(first, series, packet), other_core, other_core)
-    three = exchange(mine, across_y, to_previous_across)
+    three = exchange(mine, to_next, to_previous_across)
     held = jnp.concatenate([came[:8], mine[:8], came[8:], mine[8:]], axis=0)
     one = exchange(held, to_owner, to_previous)
     two = exchange(held, to_owner_across, across_high)

time: 29.4 us -> 27.6 us (0.939)
  starting transfers between devices: 16.6 us -> 14.5 us
  waiting for transfers between devices: 7.26 us -> 7.6 us
    ppermute x8, starting transfers between devices: 16.6 us -> 14.5 us  [exchange(): return lax.ppermute(value, ('tm', 'sta'), pairs)]
    ppermute x8, waiting for transfers between devices: 7.26 us -> 7.6 us  [exchange(): return lax.ppermute(value, ('tm', 'sta'), pairs)]
where the time goes in v5:
time: 27.6 us; the launch traced here: 27.5 us
  starting transfers between devices  14.5 us (53%)
  waiting for transfers between devices  7.6 us (28%)
  Pallas kernels  4.3 us (16%)
  other arithmetic  0.77 us (3%)
    ppermute x8, starting transfers between devices, exchange(): return lax.ppermute(value, ('tm', 'sta'), pairs)  14.5 us
    ppermute x8, waiting for transfers between devices, exchange(): return lax.ppermute(value, ('tm', 'sta'), pairs)  7.6 us
    pallas_call x1, Pallas kernels, local(): pl.pallas_call(kernel, out_shape=jax.ShapeDtypeStruct((16, 512), jnp.floa...  3.55 us
    pallas_call x1, Pallas kernels, brought(): pl.pallas_call(bring, out_shape=[pltpu.VMEM(value.shape, value.dtype) for...  0.75 us
  transfers between devices with their start and end apart: 8, of which 5 were waited for; matrix products, arithmetic and copies ran while one was open for 2% of the time, Pallas kernels for 0%

profile of v5, /device:TPU:1, one launch (start us, length us, event | category | flops | bytes accessed | tf_op | source)
XLA Modules:
  0.0 27.5 jit_solution(8124833462712616316)
XLA Ops:
  0.0 0.7 %shard_map.37 = (bf16[3,2,512]{2,1,0:T(2,128)(2,1)S(1)}, bf16[8,3,2,200]{3,2,1,0:T(2,128)(2,1)S(1)}, s32[2,128]{1,0:T(2,128)S(1)}) custom-call(bf16[3,2,512]{2,1,0:T(2,128)(2,1)} %bitcast.22, bf16[8,3,2,200]{3,2,1,0:T(2,128)(2,1)} %bitcast.21, s32[2,128]{1,0:T(2,128)} %bitcast.23), custom_call_target="tpu_custom_call" | custom-call | tf_op jit(solution)/shard_map/pallas_call | solution.py:180
  0.8 0.1 reshape.7
  0.9 1.5 %collective-permute-start = (bf16[16,640]{1,0:T(8,128)(2,1)S(1)}, bf16[16,640]{1,0:T(8,128)(2,1)S(1)}, u32[]{:S(2)}, u32[]{:S(2)}) collective-permute-start(bf16[16,640]{1,0:T(8,128)(2,1)S(1)} %get-tuple-element.18), channel_id=1, source_target_pairs={{0,8},{1,9},{2,10},{3,11},{4,12},{5,13},{6,14},{7,15},{8,0},{9,1},... | collective-permute-start | bytes 61448 | tf_op jit(solution)/shard_map/ppermute | solution.py:33
  2.4 1.4 %collective-permute-start.3 = (bf16[16,640]{1,0:T(8,128)(2,1)S(1)}, bf16[16,640]{1,0:T(8,128)(2,1)S(1)}, u32[]{:S(2)}, u32[]{:S(2)}) collective-permute-start(bf16[16,640]{1,0:T(8,128)(2,1)S(1)} %get-tuple-element.19), channel_id=1, source_target_pairs={{0,8},{1,9},{2,10},{3,11},{4,12},{5,13},{6,14},{7,15},{8,24},{9,25... | collective-permute-start | bytes 61448 | tf_op jit(solution)/shard_map/ppermute | solution.py:33
  3.8 0.0 collective-permute-done
  3.9 3.3 %collective-permute-start.2 = (bf16[32,640]{1,0:T(8,128)(2,1)S(1)}, bf16[32,640]{1,0:T(8,128)(2,1)S(1)}, u32[]{:S(2)}, u32[]{:S(2)}) collective-permute-start(bf16[32,640]{1,0:T(8,128)(2,1)S(1)} %pad_maximum_fusion.4), channel_id=1, source_target_pairs={{0,4},{1,5},{2,6},{3,7},{4,0},{5,1},{6,2},{7,3},{8,88},{9,120},{10... | collective-permute-start | bytes 122888 | tf_op jit(solution)/shard_map/ppermute | solution.py:33
  7.2 2.0 %collective-permute-start.1 = (bf16[32,640]{1,0:T(8,128)(2,1)S(1)}, bf16[32,640]{1,0:T(8,128)(2,1)S(1)}, u32[]{:S(2)}, u32[]{:S(2)}) collective-permute-start(bf16[32,640]{1,0:T(8,128)(2,1)S(1)} %pad_maximum_fusion.4), channel_id=1, source_target_pairs={{0,112},{1,113},{2,114},{3,115},{4,116},{5,117},{6,118},{7,119},{8... | collective-permute-start | bytes 122888 | tf_op jit(solution)/shard_map/ppermute | solution.py:33
  9.2 0.0 collective-permute-done.3
  9.2 2.1 %collective-permute-done.2 = bf16[32,640]{1,0:T(8,128)(2,1)S(1)} collective-permute-done((bf16[32,640]{1,0:T(8,128)(2,1)S(1)}, bf16[32,640]{1,0:T(8,128)(2,1)S(1)}, u32[]{:S(2)}, u32[]{:S(2)}) %collective-permute-start.2) | collective-permute-done | bytes 40992 | tf_op jit(solution)/shard_map/ppermute | solution.py:33
  11.4 0.4 %collective-permute-done.1 = bf16[32,640]{1,0:T(8,128)(2,1)S(1)} collective-permute-done((bf16[32,640]{1,0:T(8,128)(2,1)S(1)}, bf16[32,640]{1,0:T(8,128)(2,1)S(1)}, u32[]{:S(2)}, u32[]{:S(2)}) %collective-permute-start.1) | collective-permute-done | bytes 40992 | tf_op jit(solution)/shard_map/ppermute | solution.py:33
  11.9 2.2 %collective-permute-start.5 = (bf16[2,32,640]{2,1,0:T(8,128)(2,1)S(1)}, bf16[2,32,640]{2,1,0:T(8,128)(2,1)S(1)}, u32[]{:S(2)}, u32[]{:S(2)}) collective-permute-start(bf16[2,32,640]{2,1,0:T(8,128)(2,1)S(1)} %get-tuple-element.14), channel_id=1, source_target_pairs={{0,2},{1,3},{2,0},{3,1},{4,6},{5,7},{6,4},{7,5},{8,72},{9,73},{10,... | collective-permute-start | bytes 245768 | tf_op jit(solution)/shard_map/ppermute | solution.py:33
  14.0 3.5 %collective-permute-start.4 = (bf16[2,32,640]{2,1,0:T(8,128)(2,1)S(1)}, bf16[2,32,640]{2,1,0:T(8,128)(2,1)S(1)}, u32[]{:S(2)}, u32[]{:S(2)}) collective-permute-start(bf16[2,32,640]{2,1,0:T(8,128)(2,1)S(1)} %get-tuple-element.14), channel_id=1, source_target_pairs={{0,3},{1,0},{2,1},{3,2},{4,7},{5,4},{6,5},{7,6},{8,104},{9,105},{1... | collective-permute-start | bytes 245768 | tf_op jit(solution)/shard_map/ppermute | solution.py:33
  17.5 0.5 %collective-permute-start.6 = (bf16[2,32,640]{2,1,0:T(8,128)(2,1)S(1)}, bf16[2,32,640]{2,1,0:T(8,128)(2,1)S(1)}, u32[]{:S(2)}, u32[]{:S(2)}) collective-permute-start(bf16[2,32,640]{2,1,0:T(8,128)(2,1)S(1)} %get-tuple-element.14), channel_id=1, source_target_pairs={{0,1},{1,2},{2,3},{3,0},{4,5},{5,6},{6,7},{7,4},{8,40},{9,41},{10,... | collective-permute-start | bytes 245768 | tf_op jit(solution)/shard_map/ppermute | solution.py:33
  18.1 0.0 collective-permute-done.5
  18.1 3.0 %collective-permute-done.4 = bf16[2,32,640]{2,1,0:T(8,128)(2,1)S(1)} collective-permute-done((bf16[2,32,640]{2,1,0:T(8,128)(2,1)S(1)}, bf16[2,32,640]{2,1,0:T(8,128)(2,1)S(1)}, u32[]{:S(2)}, u32[]{:S(2)}) %collective-permute-start.4) | collective-permute-done | bytes 81952 | tf_op jit(solution)/shard_map/ppermute | solution.py:33
  21.0 1.0 %collective-permute-done.6 = bf16[2,32,640]{2,1,0:T(8,128)(2,1)S(1)} collective-permute-done((bf16[2,32,640]{2,1,0:T(8,128)(2,1)S(1)}, bf16[2,32,640]{2,1,0:T(8,128)(2,1)S(1)}, u32[]{:S(2)}, u32[]{:S(2)}) %collective-permute-start.6) | collective-permute-done | bytes 81952 | tf_op jit(solution)/shard_map/ppermute | solution.py:33
  22.0 0.1 fusion.22
  22.1 0.1 collective-permute-start.7
  22.2 0.5 %select_convert_fusion.arrangement_ref = bf16[640,1024]{1,0:T(8,128)(2,1)S(1)} fusion(s32[1024]{0:T(1024)S(1)} %get-tuple-element.24, s32[1024]{0:T(1024)S(1)} %get-tuple-element.27, s32[1024]{0:T(1024)S(1)} %get-tuple-element.25, s32[1024]{0:T(1024)S(1)} %get-tuple-element.26, pred[1024]{0:T(1024)(128)(4,1)S(1)} %get-tuple-element.28, ...), kind=kLoop, calls=%fused_computation.16 | loop fusion | flops 21626880 | bytes 1329152 | tf_op jit(solution)/shard_map/convert_element_type | solution.py:100
  22.8 1.1 %collective-permute-done.7 = bf16[4,2,32,640]{3,2,1,0:T(8,128)(2,1)S(1)} collective-permute-done((bf16[4,2,32,640]{3,2,1,0:T(8,128)(2,1)S(1)}, bf16[4,2,32,640]{3,2,1,0:T(8,128)(2,1)S(1)}, u32[]{:S(2)}, u32[]{:S(2)}) %collective-permute-start.7) | collective-permute-done | bytes 327712 | tf_op jit(solution)/shard_map/ppermute | solution.py:33
  23.8 0.1 pad_maximum_fusion.gathered_ref
  23.9 3.6 %shard_map.38 = f32[16,512]{1,0:T(8,128)} custom-call(bf16[2,4,2,32,640]{4,3,2,1,0:T(8,128)(2,1)S(1)} %pad_maximum_fusion.gathered_ref, bf16[640,1024]{1,0:T(8,128)(2,1)S(1)} %select_convert_fusion.arrangement_ref), custom_call_target="tpu_custom_call" | custom-call | flops 213811200 | bytes 600000 | tf_op jit(solution)/shard_map/pallas_call | solution.py:214
  (16 shorter events, 0.1 us)
Async XLA Ops:
  0.9 2.9 %collective-permute-start = (bf16[16,640]{1,0:T(8,128)(2,1)S(1)}, bf16[16,640]{1,0:T(8,128)(2,1)S(1)}, u32[]{:S(2)}, u32[]{:S(2)}) collective-permute-start(bf16[16,640]{1,0:T(8,128)(2,1)S(1)} %get-tuple-element.18), channel_id=1, source_target_pairs={{0,8},{1,9},{2,10},{3,11},{4,12},{5,13},{6,14},{7,15},{8,0},{9,1},... | collective-permute-start | bytes 61448 | tf_op jit(solution)/shard_map/ppermute | solution.py:33
  2.4 6.8 %collective-permute-start.3 = (bf16[16,640]{1,0:T(8,128)(2,1)S(1)}, bf16[16,640]{1,0:T(8,128)(2,1)S(1)}, u32[]{:S(2)}, u32[]{:S(2)}) collective-permute-start(bf16[16,640]{1,0:T(8,128)(2,1)S(1)} %get-tuple-element.19), channel_id=1, source_target_pairs={{0,8},{1,9},{2,10},{3,11},{4,12},{5,13},{6,14},{7,15},{8,24},{9,25... | collective-permute-start | bytes 61448 | tf_op jit(solution)/shard_map/ppermute | solution.py:33
  3.9 7.5 %collective-permute-start.2 = (bf16[32,640]{1,0:T(8,128)(2,1)S(1)}, bf16[32,640]{1,0:T(8,128)(2,1)S(1)}, u32[]{:S(2)}, u32[]{:S(2)}) collective-permute-start(bf16[32,640]{1,0:T(8,128)(2,1)S(1)} %pad_maximum_fusion.4), channel_id=1, source_target_pairs={{0,4},{1,5},{2,6},{3,7},{4,0},{5,1},{6,2},{7,3},{8,88},{9,120},{10... | collective-permute-start | bytes 122888 | tf_op jit(solution)/shard_map/ppermute | solution.py:33
  7.2 4.6 %collective-permute-start.1 = (bf16[32,640]{1,0:T(8,128)(2,1)S(1)}, bf16[32,640]{1,0:T(8,128)(2,1)S(1)}, u32[]{:S(2)}, u32[]{:S(2)}) collective-permute-start(bf16[32,640]{1,0:T(8,128)(2,1)S(1)} %pad_maximum_fusion.4), channel_id=1, source_target_pairs={{0,112},{1,113},{2,114},{3,115},{4,116},{5,117},{6,118},{7,119},{8... | collective-permute-start | bytes 122888 | tf_op jit(solution)/shard_map/ppermute | solution.py:33
  11.9 6.2 %collective-permute-start.5 = (bf16[2,32,640]{2,1,0:T(8,128)(2,1)S(1)}, bf16[2,32,640]{2,1,0:T(8,128)(2,1)S(1)}, u32[]{:S(2)}, u32[]{:S(2)}) collective-permute-start(bf16[2,32,640]{2,1,0:T(8,128)(2,1)S(1)} %get-tuple-element.14), channel_id=1, source_target_pairs={{0,2},{1,3},{2,0},{3,1},{4,6},{5,7},{6,4},{7,5},{8,72},{9,73},{10,... | collective-permute-start | bytes 245768 | tf_op jit(solution)/shard_map/ppermute | solution.py:33
  14.0 7.0 %collective-permute-start.4 = (bf16[2,32,640]{2,1,0:T(8,128)(2,1)S(1)}, bf16[2,32,640]{2,1,0:T(8,128)(2,1)S(1)}, u32[]{:S(2)}, u32[]{:S(2)}) collective-permute-start(bf16[2,32,640]{2,1,0:T(8,128)(2,1)S(1)} %get-tuple-element.14), channel_id=1, source_target_pairs={{0,3},{1,0},{2,1},{3,2},{4,7},{5,4},{6,5},{7,6},{8,104},{9,105},{1... | collective-permute-start | bytes 245768 | tf_op jit(solution)/shard_map/ppermute | solution.py:33
  17.5 4.5 %collective-permute-start.6 = (bf16[2,32,640]{2,1,0:T(8,128)(2,1)S(1)}, bf16[2,32,640]{2,1,0:T(8,128)(2,1)S(1)}, u32[]{:S(2)}, u32[]{:S(2)}) collective-permute-start(bf16[2,32,640]{2,1,0:T(8,128)(2,1)S(1)} %get-tuple-element.14), channel_id=1, source_target_pairs={{0,1},{1,2},{2,3},{3,0},{4,5},{5,6},{6,7},{7,4},{8,40},{9,41},{10,... | collective-permute-start | bytes 245768 | tf_op jit(solution)/shard_map/ppermute | solution.py:33
  22.1 1.7 %collective-permute-start.7 = (bf16[4,2,32,640]{3,2,1,0:T(8,128)(2,1)S(1)}, bf16[4,2,32,640]{3,2,1,0:T(8,128)(2,1)S(1)}, u32[]{:S(2)}, u32[]{:S(2)}) collective-permute-start(bf16[4,2,32,640]{3,2,1,0:T(8,128)(2,1)S(1)} %get-tuple-element.12), channel_id=1, source_target_pairs={{0,8},{1,9},{2,10},{3,11},{4,12},{5,13},{6,14},{7,15},{8,0},{9,1},... | collective-permute-start | bytes 983048 | tf_op jit(solution)/shard_map/ppermute | solution.py:33

commit v6 on v5

--- a/solution.py
+++ b/solution.py
@@ -109,7 +109,7 @@
     own = lane == template + 16 * j
     energies = []
     for slot in range(8):
-        level = lax.rem(x + slot // 2 - j // 2 + 6, 4)
+        level = lax.rem(x - slot // 2 - j // 2 + 10, 4)
         half = lax.rem(y + slot % 2 + j, 2)
         held = gathered_ref[1 - sender, level, half].astype(jnp.float32)
         pieces = [held[at : at + ROWS, :512] for at in (0, 8, 16)]
@@ -208,7 +208,7 @@
     near = jnp.where(first, one, jnp.concatenate([mine[:8], came[:8], near_after, mine[8:]], axis=0))
     far = jnp.where(first, two, jnp.concatenate([two[8:16], two[:8], far_after, two[24:]], axis=0))
     held = jnp.stack([near, far])
-    held = jnp.stack([held] + [exchange(held, back_x(steps), back_z(steps)) for steps in (1, 2, 3)])
+    held = jnp.stack([held] + [exchange(held, back_x(-steps), back_z(steps)) for steps in (1, 2, 3)])
     held = jnp.stack([held, exchange(held, other_core, other_core)])
 
     return pl.pallas_call(

time: 27.6 us -> 27.1 us (0.982)
  waiting for transfers between devices: 7.6 us -> 6.72 us
  starting transfers between devices: 14.5 us -> 14.9 us
    ppermute x8, waiting for transfers between devices: 7.6 us -> 6.72 us  [exchange(): return lax.ppermute(value, ('tm', 'sta'), pairs)]
    ppermute x8, starting transfers between devices: 14.5 us -> 14.9 us  [exchange(): return lax.ppermute(value, ('tm', 'sta'), pairs)]
where the time goes in v6:
time: 27.1 us; the launch traced here: 26.9 us
  starting transfers between devices  14.9 us (55%)
  waiting for transfers between devices  6.72 us (25%)
  Pallas kernels  4.3 us (16%)
  other arithmetic  0.75 us (3%)
    ppermute x8, starting transfers between devices, exchange(): return lax.ppermute(value, ('tm', 'sta'), pairs)  14.9 us
    ppermute x8, waiting for transfers between devices, exchange(): return lax.ppermute(value, ('tm', 'sta'), pairs)  6.72 us
    pallas_call x1, Pallas kernels, local(): pl.pallas_call(kernel, out_shape=jax.ShapeDtypeStruct((16, 512), jnp.floa...  3.55 us
    pallas_call x1, Pallas kernels, brought(): pl.pallas_call(bring, out_shape=[pltpu.VMEM(value.shape, value.dtype) for...  0.75 us
  transfers between devices with their start and end apart: 8, of which 5 were waited for; matrix products, arithmetic and copies ran while one was open for 2% of the time, Pallas kernels for 0%

profile of v6, /device:TPU:1, one launch (start us, length us, event | category | flops | bytes accessed | tf_op | source)
XLA Modules:
  0.0 26.9 jit_solution(1664568712056139556)
XLA Ops:
  0.0 0.7 %shard_map.37 = (bf16[3,2,512]{2,1,0:T(2,128)(2,1)S(1)}, bf16[8,3,2,200]{3,2,1,0:T(2,128)(2,1)S(1)}, s32[2,128]{1,0:T(2,128)S(1)}) custom-call(bf16[3,2,512]{2,1,0:T(2,128)(2,1)} %bitcast.22, bf16[8,3,2,200]{3,2,1,0:T(2,128)(2,1)} %bitcast.21, s32[2,128]{1,0:T(2,128)} %bitcast.23), custom_call_target="tpu_custom_call" | custom-call | tf_op jit(solution)/shard_map/pallas_call | solution.py:180
  0.8 0.1 reshape.7
  0.9 1.5 %collective-permute-start = (bf16[16,640]{1,0:T(8,128)(2,1)S(1)}, bf16[16,640]{1,0:T(8,128)(2,1)S(1)}, u32[]{:S(2)}, u32[]{:S(2)}) collective-permute-start(bf16[16,640]{1,0:T(8,128)(2,1)S(1)} %get-tuple-element.18), channel_id=1, source_target_pairs={{0,8},{1,9},{2,10},{3,11},{4,12},{5,13},{6,14},{7,15},{8,0},{9,1},... | collective-permute-start | bytes 61448 | tf_op jit(solution)/shard_map/ppermute | solution.py:33
  2.4 1.4 %collective-permute-start.3 = (bf16[16,640]{1,0:T(8,128)(2,1)S(1)}, bf16[16,640]{1,0:T(8,128)(2,1)S(1)}, u32[]{:S(2)}, u32[]{:S(2)}) collective-permute-start(bf16[16,640]{1,0:T(8,128)(2,1)S(1)} %get-tuple-element.19), channel_id=1, source_target_pairs={{0,8},{1,9},{2,10},{3,11},{4,12},{5,13},{6,14},{7,15},{8,24},{9,25... | collective-permute-start | bytes 61448 | tf_op jit(solution)/shard_map/ppermute | solution.py:33
  3.8 0.0 collective-permute-done
  3.9 3.3 %collective-permute-start.2 = (bf16[32,640]{1,0:T(8,128)(2,1)S(1)}, bf16[32,640]{1,0:T(8,128)(2,1)S(1)}, u32[]{:S(2)}, u32[]{:S(2)}) collective-permute-start(bf16[32,640]{1,0:T(8,128)(2,1)S(1)} %pad_maximum_fusion.4), channel_id=1, source_target_pairs={{0,4},{1,5},{2,6},{3,7},{4,0},{5,1},{6,2},{7,3},{8,88},{9,120},{10... | collective-permute-start | bytes 122888 | tf_op jit(solution)/shard_map/ppermute | solution.py:33
  7.2 2.0 %collective-permute-start.1 = (bf16[32,640]{1,0:T(8,128)(2,1)S(1)}, bf16[32,640]{1,0:T(8,128)(2,1)S(1)}, u32[]{:S(2)}, u32[]{:S(2)}) collective-permute-start(bf16[32,640]{1,0:T(8,128)(2,1)S(1)} %pad_maximum_fusion.4), channel_id=1, source_target_pairs={{0,112},{1,113},{2,114},{3,115},{4,116},{5,117},{6,118},{7,119},{8... | collective-permute-start | bytes 122888 | tf_op jit(solution)/shard_map/ppermute | solution.py:33
  9.2 0.0 collective-permute-done.3
  9.2 2.1 %collective-permute-done.2 = bf16[32,640]{1,0:T(8,128)(2,1)S(1)} collective-permute-done((bf16[32,640]{1,0:T(8,128)(2,1)S(1)}, bf16[32,640]{1,0:T(8,128)(2,1)S(1)}, u32[]{:S(2)}, u32[]{:S(2)}) %collective-permute-start.2) | collective-permute-done | bytes 40992 | tf_op jit(solution)/shard_map/ppermute | solution.py:33
  11.4 0.4 %collective-permute-done.1 = bf16[32,640]{1,0:T(8,128)(2,1)S(1)} collective-permute-done((bf16[32,640]{1,0:T(8,128)(2,1)S(1)}, bf16[32,640]{1,0:T(8,128)(2,1)S(1)}, u32[]{:S(2)}, u32[]{:S(2)}) %collective-permute-start.1) | collective-permute-done | bytes 40992 | tf_op jit(solution)/shard_map/ppermute | solution.py:33
  11.9 2.2 %collective-permute-start.5 = (bf16[2,32,640]{2,1,0:T(8,128)(2,1)S(1)}, bf16[2,32,640]{2,1,0:T(8,128)(2,1)S(1)}, u32[]{:S(2)}, u32[]{:S(2)}) collective-permute-start(bf16[2,32,640]{2,1,0:T(8,128)(2,1)S(1)} %get-tuple-element.14), channel_id=1, source_target_pairs={{0,2},{1,3},{2,0},{3,1},{4,6},{5,7},{6,4},{7,5},{8,72},{9,73},{10,... | collective-permute-start | bytes 245768 | tf_op jit(solution)/shard_map/ppermute | solution.py:33
  14.0 4.0 %collective-permute-start.4 = (bf16[2,32,640]{2,1,0:T(8,128)(2,1)S(1)}, bf16[2,32,640]{2,1,0:T(8,128)(2,1)S(1)}, u32[]{:S(2)}, u32[]{:S(2)}) collective-permute-start(bf16[2,32,640]{2,1,0:T(8,128)(2,1)S(1)} %get-tuple-element.14), channel_id=1, source_target_pairs={{0,3},{1,0},{2,1},{3,2},{4,7},{5,4},{6,5},{7,6},{8,40},{9,41},{10,... | collective-permute-start | bytes 245768 | tf_op jit(solution)/shard_map/ppermute | solution.py:33
  18.0 0.0 collective-permute-start.6
  18.1 0.0 collective-permute-done.5
  18.1 1.5 %collective-permute-done.4 = bf16[2,32,640]{2,1,0:T(8,128)(2,1)S(1)} collective-permute-done((bf16[2,32,640]{2,1,0:T(8,128)(2,1)S(1)}, bf16[2,32,640]{2,1,0:T(8,128)(2,1)S(1)}, u32[]{:S(2)}, u32[]{:S(2)}) %collective-permute-start.4) | collective-permute-done | bytes 81952 | tf_op jit(solution)/shard_map/ppermute | solution.py:33
  19.5 2.0 %collective-permute-done.6 = bf16[2,32,640]{2,1,0:T(8,128)(2,1)S(1)} collective-permute-done((bf16[2,32,640]{2,1,0:T(8,128)(2,1)S(1)}, bf16[2,32,640]{2,1,0:T(8,128)(2,1)S(1)}, u32[]{:S(2)}, u32[]{:S(2)}) %collective-permute-start.6) | collective-permute-done | bytes 81952 | tf_op jit(solution)/shard_map/ppermute | solution.py:33
  21.5 0.1 fusion.22
  21.6 0.5 %collective-permute-start.7 = (bf16[4,2,32,640]{3,2,1,0:T(8,128)(2,1)S(1)}, bf16[4,2,32,640]{3,2,1,0:T(8,128)(2,1)S(1)}, u32[]{:S(2)}, u32[]{:S(2)}) collective-permute-start(bf16[4,2,32,640]{3,2,1,0:T(8,128)(2,1)S(1)} %get-tuple-element.12), channel_id=1, source_target_pairs={{0,8},{1,9},{2,10},{3,11},{4,12},{5,13},{6,14},{7,15},{8,0},{9,1},... | collective-permute-start | bytes 983048 | tf_op jit(solution)/shard_map/ppermute | solution.py:33
  22.1 0.5 %select_convert_fusion.arrangement_ref = bf16[640,1024]{1,0:T(8,128)(2,1)S(1)} fusion(s32[1024]{0:T(1024)S(1)} %get-tuple-element.24, s32[1024]{0:T(1024)S(1)} %get-tuple-element.27, s32[1024]{0:T(1024)S(1)} %get-tuple-element.25, s32[1024]{0:T(1024)S(1)} %get-tuple-element.26, pred[1024]{0:T(1024)(128)(4,1)S(1)} %get-tuple-element.28, ...), kind=kLoop, calls=%fused_computation.16 | loop fusion | flops 21626880 | bytes 1329152 | tf_op jit(solution)/shard_map/convert_element_type | solution.py:100
  22.6 0.7 %collective-permute-done.7 = bf16[4,2,32,640]{3,2,1,0:T(8,128)(2,1)S(1)} collective-permute-done((bf16[4,2,32,640]{3,2,1,0:T(8,128)(2,1)S(1)}, bf16[4,2,32,640]{3,2,1,0:T(8,128)(2,1)S(1)}, u32[]{:S(2)}, u32[]{:S(2)}) %collective-permute-start.7) | collective-permute-done | bytes 327712 | tf_op jit(solution)/shard_map/ppermute | solution.py:33
  23.3 0.1 pad_maximum_fusion.gathered_ref
  23.4 3.5 %shard_map.38 = f32[16,512]{1,0:T(8,128)} custom-call(bf16[2,4,2,32,640]{4,3,2,1,0:T(8,128)(2,1)S(1)} %pad_maximum_fusion.gathered_ref, bf16[640,1024]{1,0:T(8,128)(2,1)S(1)} %select_convert_fusion.arrangement_ref), custom_call_target="tpu_custom_call" | custom-call | flops 213811200 | bytes 600000 | tf_op jit(solution)/shard_map/pallas_call | solution.py:214
  (16 shorter events, 0.1 us)
Async XLA Ops:
  0.9 2.9 %collective-permute-start = (bf16[16,640]{1,0:T(8,128)(2,1)S(1)}, bf16[16,640]{1,0:T(8,128)(2,1)S(1)}, u32[]{:S(2)}, u32[]{:S(2)}) collective-permute-start(bf16[16,640]{1,0:T(8,128)(2,1)S(1)} %get-tuple-element.18), channel_id=1, source_target_pairs={{0,8},{1,9},{2,10},{3,11},{4,12},{5,13},{6,14},{7,15},{8,0},{9,1},... | collective-permute-start | bytes 61448 | tf_op jit(solution)/shard_map/ppermute | solution.py:33
  2.4 6.8 %collective-permute-start.3 = (bf16[16,640]{1,0:T(8,128)(2,1)S(1)}, bf16[16,640]{1,0:T(8,128)(2,1)S(1)}, u32[]{:S(2)}, u32[]{:S(2)}) collective-permute-start(bf16[16,640]{1,0:T(8,128)(2,1)S(1)} %get-tuple-element.19), channel_id=1, source_target_pairs={{0,8},{1,9},{2,10},{3,11},{4,12},{5,13},{6,14},{7,15},{8,24},{9,25... | collective-permute-start | bytes 61448 | tf_op jit(solution)/shard_map/ppermute | solution.py:33
  3.9 7.5 %collective-permute-start.2 = (bf16[32,640]{1,0:T(8,128)(2,1)S(1)}, bf16[32,640]{1,0:T(8,128)(2,1)S(1)}, u32[]{:S(2)}, u32[]{:S(2)}) collective-permute-start(bf16[32,640]{1,0:T(8,128)(2,1)S(1)} %pad_maximum_fusion.4), channel_id=1, source_target_pairs={{0,4},{1,5},{2,6},{3,7},{4,0},{5,1},{6,2},{7,3},{8,88},{9,120},{10... | collective-permute-start | bytes 122888 | tf_op jit(solution)/shard_map/ppermute | solution.py:33
  7.2 4.6 %collective-permute-start.1 = (bf16[32,640]{1,0:T(8,128)(2,1)S(1)}, bf16[32,640]{1,0:T(8,128)(2,1)S(1)}, u32[]{:S(2)}, u32[]{:S(2)}) collective-permute-start(bf16[32,640]{1,0:T(8,128)(2,1)S(1)} %pad_maximum_fusion.4), channel_id=1, source_target_pairs={{0,112},{1,113},{2,114},{3,115},{4,116},{5,117},{6,118},{7,119},{8... | collective-permute-start | bytes 122888 | tf_op jit(solution)/shard_map/ppermute | solution.py:33
  11.9 6.2 %collective-permute-start.5 = (bf16[2,32,640]{2,1,0:T(8,128)(2,1)S(1)}, bf16[2,32,640]{2,1,0:T(8,128)(2,1)S(1)}, u32[]{:S(2)}, u32[]{:S(2)}) collective-permute-start(bf16[2,32,640]{2,1,0:T(8,128)(2,1)S(1)} %get-tuple-element.14), channel_id=1, source_target_pairs={{0,2},{1,3},{2,0},{3,1},{4,6},{5,7},{6,4},{7,5},{8,72},{9,73},{10,... | collective-permute-start | bytes 245768 | tf_op jit(solution)/shard_map/ppermute | solution.py:33
  14.0 5.5 %collective-permute-start.4 = (bf16[2,32,640]{2,1,0:T(8,128)(2,1)S(1)}, bf16[2,32,640]{2,1,0:T(8,128)(2,1)S(1)}, u32[]{:S(2)}, u32[]{:S(2)}) collective-permute-start(bf16[2,32,640]{2,1,0:T(8,128)(2,1)S(1)} %get-tuple-element.14), channel_id=1, source_target_pairs={{0,3},{1,0},{2,1},{3,2},{4,7},{5,4},{6,5},{7,6},{8,40},{9,41},{10,... | collective-permute-start | bytes 245768 | tf_op jit(solution)/shard_map/ppermute | solution.py:33
  18.0 3.5 %collective-permute-start.6 = (bf16[2,32,640]{2,1,0:T(8,128)(2,1)S(1)}, bf16[2,32,640]{2,1,0:T(8,128)(2,1)S(1)}, u32[]{:S(2)}, u32[]{:S(2)}) collective-permute-start(bf16[2,32,640]{2,1,0:T(8,128)(2,1)S(1)} %get-tuple-element.14), channel_id=1, source_target_pairs={{0,1},{1,2},{2,3},{3,0},{4,5},{5,6},{6,7},{7,4},{8,104},{9,105},{1... | collective-permute-start | bytes 245768 | tf_op jit(solution)/shard_map/ppermute | solution.py:33
  21.6 1.7 %collective-permute-start.7 = (bf16[4,2,32,640]{3,2,1,0:T(8,128)(2,1)S(1)}, bf16[4,2,32,640]{3,2,1,0:T(8,128)(2,1)S(1)}, u32[]{:S(2)}, u32[]{:S(2)}) collective-permute-start(bf16[4,2,32,640]{3,2,1,0:T(8,128)(2,1)S(1)} %get-tuple-element.12), channel_id=1, source_target_pairs={{0,8},{1,9},{2,10},{3,11},{4,12},{5,13},{6,14},{7,15},{8,0},{9,1},... | collective-permute-start | bytes 983048 | tf_op jit(solution)/shard_map/ppermute | solution.py:33

commit v7 on v6

--- a/solution.py
+++ b/solution.py
@@ -109,7 +109,7 @@
     own = lane == template + 16 * j
     energies = []
     for slot in range(8):
-        level = lax.rem(x - slot // 2 - j // 2 + 10, 4)
+        level = lax.rem(j // 2 - x + slot // 2 + 6, 4)
         half = lax.rem(y + slot % 2 + j, 2)
         held = gathered_ref[1 - sender, level, half].astype(jnp.float32)
         pieces = [held[at : at + ROWS, :512] for at in (0, 8, 16)]
@@ -208,7 +208,7 @@
     near = jnp.where(first, one, jnp.concatenate([mine[:8], came[:8], near_after, mine[8:]], axis=0))
     far = jnp.where(first, two, jnp.concatenate([two[8:16], two[:8], far_after, two[24:]], axis=0))
     held = jnp.stack([near, far])
-    held = jnp.stack([held] + [exchange(held, back_x(-steps), back_z(steps)) for steps in (1, 2, 3)])
+    held = jnp.stack([held] + [exchange(held, back_x(-steps), back_z(-steps)) for steps in (1, 2, 3)])
     held = jnp.stack([held, exchange(held, other_core, other_core)])
 
     return pl.pallas_call(

time: 27.1 us -> 26.9 us (level)
  no operation moved by 1% of the time
where the time goes in v7:
time: 26.9 us; the launch traced here: 26.7 us
  starting transfers between devices  14.7 us (55%)
  waiting for transfers between devices  6.72 us (25%)
  Pallas kernels  4.3 us (16%)
  other arithmetic  0.75 us (3%)
    ppermute x8, starting transfers between devices, exchange(): return lax.ppermute(value, ('tm', 'sta'), pairs)  14.7 us
    ppermute x8, waiting for transfers between devices, exchange(): return lax.ppermute(value, ('tm', 'sta'), pairs)  6.72 us
    pallas_call x1, Pallas kernels, local(): pl.pallas_call(kernel, out_shape=jax.ShapeDtypeStruct((16, 512), jnp.floa...  3.56 us
    pallas_call x1, Pallas kernels, brought(): pl.pallas_call(bring, out_shape=[pltpu.VMEM(value.shape, value.dtype) for...  0.75 us
  transfers between devices with their start and end apart: 8, of which 5 were waited for; matrix products, arithmetic and copies ran while one was open for 2% of the time, Pallas kernels for 0%

profile of v7, /device:TPU:1, one launch (start us, length us, event | category | flops | bytes accessed | tf_op | source)
XLA Modules:
  0.0 26.7 jit_solution(2996094135355826149)
XLA Ops:
  0.0 0.7 %shard_map.37 = (bf16[3,2,512]{2,1,0:T(2,128)(2,1)S(1)}, bf16[8,3,2,200]{3,2,1,0:T(2,128)(2,1)S(1)}, s32[2,128]{1,0:T(2,128)S(1)}) custom-call(bf16[3,2,512]{2,1,0:T(2,128)(2,1)} %bitcast.22, bf16[8,3,2,200]{3,2,1,0:T(2,128)(2,1)} %bitcast.21, s32[2,128]{1,0:T(2,128)} %bitcast.23), custom_call_target="tpu_custom_call" | custom-call | tf_op jit(solution)/shard_map/pallas_call | solution.py:180
  0.8 0.1 reshape.7
  0.9 1.5 %collective-permute-start = (bf16[16,640]{1,0:T(8,128)(2,1)S(1)}, bf16[16,640]{1,0:T(8,128)(2,1)S(1)}, u32[]{:S(2)}, u32[]{:S(2)}) collective-permute-start(bf16[16,640]{1,0:T(8,128)(2,1)S(1)} %get-tuple-element.18), channel_id=1, source_target_pairs={{0,8},{1,9},{2,10},{3,11},{4,12},{5,13},{6,14},{7,15},{8,0},{9,1},... | collective-permute-start | bytes 61448 | tf_op jit(solution)/shard_map/ppermute | solution.py:33
  2.4 1.4 %collective-permute-start.3 = (bf16[16,640]{1,0:T(8,128)(2,1)S(1)}, bf16[16,640]{1,0:T(8,128)(2,1)S(1)}, u32[]{:S(2)}, u32[]{:S(2)}) collective-permute-start(bf16[16,640]{1,0:T(8,128)(2,1)S(1)} %get-tuple-element.19), channel_id=1, source_target_pairs={{0,8},{1,9},{2,10},{3,11},{4,12},{5,13},{6,14},{7,15},{8,24},{9,25... | collective-permute-start | bytes 61448 | tf_op jit(solution)/shard_map/ppermute | solution.py:33
  3.8 0.0 collective-permute-done
  3.9 3.3 %collective-permute-start.2 = (bf16[32,640]{1,0:T(8,128)(2,1)S(1)}, bf16[32,640]{1,0:T(8,128)(2,1)S(1)}, u32[]{:S(2)}, u32[]{:S(2)}) collective-permute-start(bf16[32,640]{1,0:T(8,128)(2,1)S(1)} %pad_maximum_fusion.4), channel_id=1, source_target_pairs={{0,4},{1,5},{2,6},{3,7},{4,0},{5,1},{6,2},{7,3},{8,88},{9,120},{10... | collective-permute-start | bytes 122888 | tf_op jit(solution)/shard_map/ppermute | solution.py:33
  7.2 2.0 %collective-permute-start.1 = (bf16[32,640]{1,0:T(8,128)(2,1)S(1)}, bf16[32,640]{1,0:T(8,128)(2,1)S(1)}, u32[]{:S(2)}, u32[]{:S(2)}) collective-permute-start(bf16[32,640]{1,0:T(8,128)(2,1)S(1)} %pad_maximum_fusion.4), channel_id=1, source_target_pairs={{0,112},{1,113},{2,114},{3,115},{4,116},{5,117},{6,118},{7,119},{8... | collective-permute-start | bytes 122888 | tf_op jit(solution)/shard_map/ppermute | solution.py:33
  9.2 0.0 collective-permute-done.3
  9.2 2.1 %collective-permute-done.2 = bf16[32,640]{1,0:T(8,128)(2,1)S(1)} collective-permute-done((bf16[32,640]{1,0:T(8,128)(2,1)S(1)}, bf16[32,640]{1,0:T(8,128)(2,1)S(1)}, u32[]{:S(2)}, u32[]{:S(2)}) %collective-permute-start.2) | collective-permute-done | bytes 40992 | tf_op jit(solution)/shard_map/ppermute | solution.py:33
  11.4 0.4 %collective-permute-done.1 = bf16[32,640]{1,0:T(8,128)(2,1)S(1)} collective-permute-done((bf16[32,640]{1,0:T(8,128)(2,1)S(1)}, bf16[32,640]{1,0:T(8,128)(2,1)S(1)}, u32[]{:S(2)}, u32[]{:S(2)}) %collective-permute-start.1) | collective-permute-done | bytes 40992 | tf_op jit(solution)/shard_map/ppermute | solution.py:33
  11.9 2.2 %collective-permute-start.5 = (bf16[2,32,640]{2,1,0:T(8,128)(2,1)S(1)}, bf16[2,32,640]{2,1,0:T(8,128)(2,1)S(1)}, u32[]{:S(2)}, u32[]{:S(2)}) collective-permute-start(bf16[2,32,640]{2,1,0:T(8,128)(2,1)S(1)} %get-tuple-element.14), channel_id=1, source_target_pairs={{0,2},{1,3},{2,0},{3,1},{4,6},{5,7},{6,4},{7,5},{8,72},{9,73},{10,... | collective-permute-start | bytes 245768 | tf_op jit(solution)/shard_map/ppermute | solution.py:33
  14.0 4.0 %collective-permute-start.4 = (bf16[2,32,640]{2,1,0:T(8,128)(2,1)S(1)}, bf16[2,32,640]{2,1,0:T(8,128)(2,1)S(1)}, u32[]{:S(2)}, u32[]{:S(2)}) collective-permute-start(bf16[2,32,640]{2,1,0:T(8,128)(2,1)S(1)} %get-tuple-element.14), channel_id=1, source_target_pairs={{0,1},{1,2},{2,3},{3,0},{4,5},{5,6},{6,7},{7,4},{8,40},{9,41},{10,... | collective-permute-start | bytes 245768 | tf_op jit(solution)/shard_map/ppermute | solution.py:33
  18.0 0.0 collective-permute-start.6
  18.1 0.0 collective-permute-done.5
  18.1 1.5 %collective-permute-done.4 = bf16[2,32,640]{2,1,0:T(8,128)(2,1)S(1)} collective-permute-done((bf16[2,32,640]{2,1,0:T(8,128)(2,1)S(1)}, bf16[2,32,640]{2,1,0:T(8,128)(2,1)S(1)}, u32[]{:S(2)}, u32[]{:S(2)}) %collective-permute-start.4) | collective-permute-done | bytes 81952 | tf_op jit(solution)/shard_map/ppermute | solution.py:33
  19.5 1.8 %collective-permute-done.6 = bf16[2,32,640]{2,1,0:T(8,128)(2,1)S(1)} collective-permute-done((bf16[2,32,640]{2,1,0:T(8,128)(2,1)S(1)}, bf16[2,32,640]{2,1,0:T(8,128)(2,1)S(1)}, u32[]{:S(2)}, u32[]{:S(2)}) %collective-permute-start.6) | collective-permute-done | bytes 81952 | tf_op jit(solution)/shard_map/ppermute | solution.py:33
  21.3 0.1 fusion.22
  21.4 0.3 collective-permute-start.7
  21.7 0.5 %select_convert_fusion.arrangement_ref = bf16[640,1024]{1,0:T(8,128)(2,1)S(1)} fusion(s32[1024]{0:T(1024)S(1)} %get-tuple-element.24, s32[1024]{0:T(1024)S(1)} %get-tuple-element.27, s32[1024]{0:T(1024)S(1)} %get-tuple-element.25, s32[1024]{0:T(1024)S(1)} %get-tuple-element.26, pred[1024]{0:T(1024)(128)(4,1)S(1)} %get-tuple-element.28, ...), kind=kLoop, calls=%fused_computation.16 | loop fusion | flops 21626880 | bytes 1329152 | tf_op jit(solution)/shard_map/convert_element_type | solution.py:100
  22.2 0.9 %collective-permute-done.7 = bf16[4,2,32,640]{3,2,1,0:T(8,128)(2,1)S(1)} collective-permute-done((bf16[4,2,32,640]{3,2,1,0:T(8,128)(2,1)S(1)}, bf16[4,2,32,640]{3,2,1,0:T(8,128)(2,1)S(1)}, u32[]{:S(2)}, u32[]{:S(2)}) %collective-permute-start.7) | collective-permute-done | bytes 327712 | tf_op jit(solution)/shard_map/ppermute | solution.py:33
  23.1 0.1 pad_maximum_fusion.gathered_ref
  23.2 3.6 %shard_map.38 = f32[16,512]{1,0:T(8,128)} custom-call(bf16[2,4,2,32,640]{4,3,2,1,0:T(8,128)(2,1)S(1)} %pad_maximum_fusion.gathered_ref, bf16[640,1024]{1,0:T(8,128)(2,1)S(1)} %select_convert_fusion.arrangement_ref), custom_call_target="tpu_custom_call" | custom-call | flops 213811200 | bytes 600000 | tf_op jit(solution)/shard_map/pallas_call | solution.py:214
  (16 shorter events, 0.1 us)
Async XLA Ops:
  0.9 2.9 %collective-permute-start = (bf16[16,640]{1,0:T(8,128)(2,1)S(1)}, bf16[16,640]{1,0:T(8,128)(2,1)S(1)}, u32[]{:S(2)}, u32[]{:S(2)}) collective-permute-start(bf16[16,640]{1,0:T(8,128)(2,1)S(1)} %get-tuple-element.18), channel_id=1, source_target_pairs={{0,8},{1,9},{2,10},{3,11},{4,12},{5,13},{6,14},{7,15},{8,0},{9,1},... | collective-permute-start | bytes 61448 | tf_op jit(solution)/shard_map/ppermute | solution.py:33
  2.4 6.8 %collective-permute-start.3 = (bf16[16,640]{1,0:T(8,128)(2,1)S(1)}, bf16[16,640]{1,0:T(8,128)(2,1)S(1)}, u32[]{:S(2)}, u32[]{:S(2)}) collective-permute-start(bf16[16,640]{1,0:T(8,128)(2,1)S(1)} %get-tuple-element.19), channel_id=1, source_target_pairs={{0,8},{1,9},{2,10},{3,11},{4,12},{5,13},{6,14},{7,15},{8,24},{9,25... | collective-permute-start | bytes 61448 | tf_op jit(solution)/shard_map/ppermute | solution.py:33
  3.9 7.5 %collective-permute-start.2 = (bf16[32,640]{1,0:T(8,128)(2,1)S(1)}, bf16[32,640]{1,0:T(8,128)(2,1)S(1)}, u32[]{:S(2)}, u32[]{:S(2)}) collective-permute-start(bf16[32,640]{1,0:T(8,128)(2,1)S(1)} %pad_maximum_fusion.4), channel_id=1, source_target_pairs={{0,4},{1,5},{2,6},{3,7},{4,0},{5,1},{6,2},{7,3},{8,88},{9,120},{10... | collective-permute-start | bytes 122888 | tf_op jit(solution)/shard_map/ppermute | solution.py:33
  7.2 4.6 %collective-permute-start.1 = (bf16[32,640]{1,0:T(8,128)(2,1)S(1)}, bf16[32,640]{1,0:T(8,128)(2,1)S(1)}, u32[]{:S(2)}, u32[]{:S(2)}) collective-permute-start(bf16[32,640]{1,0:T(8,128)(2,1)S(1)} %pad_maximum_fusion.4), channel_id=1, source_target_pairs={{0,112},{1,113},{2,114},{3,115},{4,116},{5,117},{6,118},{7,119},{8... | collective-permute-start | bytes 122888 | tf_op jit(solution)/shard_map/ppermute | solution.py:33
  11.9 6.2 %collective-permute-start.5 = (bf16[2,32,640]{2,1,0:T(8,128)(2,1)S(1)}, bf16[2,32,640]{2,1,0:T(8,128)(2,1)S(1)}, u32[]{:S(2)}, u32[]{:S(2)}) collective-permute-start(bf16[2,32,640]{2,1,0:T(8,128)(2,1)S(1)} %get-tuple-element.14), channel_id=1, source_target_pairs={{0,2},{1,3},{2,0},{3,1},{4,6},{5,7},{6,4},{7,5},{8,72},{9,73},{10,... | collective-permute-start | bytes 245768 | tf_op jit(solution)/shard_map/ppermute | solution.py:33
  14.0 5.5 %collective-permute-start.4 = (bf16[2,32,640]{2,1,0:T(8,128)(2,1)S(1)}, bf16[2,32,640]{2,1,0:T(8,128)(2,1)S(1)}, u32[]{:S(2)}, u32[]{:S(2)}) collective-permute-start(bf16[2,32,640]{2,1,0:T(8,128)(2,1)S(1)} %get-tuple-element.14), channel_id=1, source_target_pairs={{0,1},{1,2},{2,3},{3,0},{4,5},{5,6},{6,7},{7,4},{8,40},{9,41},{10,... | collective-permute-start | bytes 245768 | tf_op jit(solution)/shard_map/ppermute | solution.py:33
  18.0 3.3 %collective-permute-start.6 = (bf16[2,32,640]{2,1,0:T(8,128)(2,1)S(1)}, bf16[2,32,640]{2,1,0:T(8,128)(2,1)S(1)}, u32[]{:S(2)}, u32[]{:S(2)}) collective-permute-start(bf16[2,32,640]{2,1,0:T(8,128)(2,1)S(1)} %get-tuple-element.14), channel_id=1, source_target_pairs={{0,3},{1,0},{2,1},{3,2},{4,7},{5,4},{6,5},{7,6},{8,104},{9,105},{1... | collective-permute-start | bytes 245768 | tf_op jit(solution)/shard_map/ppermute | solution.py:33
  21.4 1.7 %collective-permute-start.7 = (bf16[4,2,32,640]{3,2,1,0:T(8,128)(2,1)S(1)}, bf16[4,2,32,640]{3,2,1,0:T(8,128)(2,1)S(1)}, u32[]{:S(2)}, u32[]{:S(2)}) collective-permute-start(bf16[4,2,32,640]{3,2,1,0:T(8,128)(2,1)S(1)} %get-tuple-element.12), channel_id=1, source_target_pairs={{0,8},{1,9},{2,10},{3,11},{4,12},{5,13},{6,14},{7,15},{8,0},{9,1},... | collective-permute-start | bytes 983048 | tf_op jit(solution)/shard_map/ppermute | solution.py:33
